TPU v7x, 256 devices: a whole 4x4x8 slice. The times are simulated.
256 devices in a mesh: dp: 16 (over z_lo, x), seq: 16 (over z_hi, y, core).
Axes of the slice: x: 4, y: 4, z: 8 (z_hi: 2, z_lo: 4; z = z_hi * 4 + z_lo), core: 2. Of those that a mesh axis runs over, the one named last changes fastest.
Arguments:
- query: bfloat16 [16, 2048, 1536], P('dp', 'seq'), may hold values from -10 to 10
- key_proj: bfloat16 [16, 2048, 1536], P('dp', 'seq'), may hold values from -10 to 10
- value: bfloat16 [16, 2048, 1536], P('dp', 'seq'), may hold values from -6 to 6
- cotangent: bfloat16 [16, 2048, 1536], P('dp', 'seq'), may hold values from -6 to 6
- out_weight: bfloat16 [1536, 1536], P(('dp', 'seq')), may hold values from -0.15625 to 0.15625
Outputs:
- projected: bfloat16 [16, 2048, 1536], P('dp', 'seq')
- grad_query: bfloat16 [16, 2048, 1536], P('dp', 'seq')
- grad_key: bfloat16 [16, 2048, 1536], P('dp', 'seq')
- grad_value: bfloat16 [16, 2048, 1536], P('dp', 'seq')
- grad_weight: float32 [1536, 1536], P(('dp', 'seq'))
All inputs are finite; a program needn't handle non-finite values.
Results may differ from a plain program's by a relative error of at most 0.015.
Values may be sent and summed in bfloat16 or wider, within the bound.
No kernel may reach another device: no remote copies, remote signals or barrier semaphores. Data moves between devices by JAX's collectives and lax.ppermute only.
A program may use at most 128 MiB of HBM per device.

v0:
```python
import math

import jax
import jax.numpy as jnp
from jax import lax
from jax.sharding import PartitionSpec as P

HD = 96


def split_heads(array_in):
    utt_count, length, feat_width = array_in.shape
    return array_in.reshape(utt_count, length, feat_width // HD, HD)


def softmax_rows(query_block, keys_four):
    factor = 1.0 / math.sqrt(HD)
    scores = (
        jnp.einsum("bqhd,bkhd->bhqk", query_block, keys_four, preferred_element_type=jnp.float32)
        * factor
    )
    top_score = jnp.max(scores, axis=3, keepdims=True)
    exp_scores = jnp.exp(scores - top_score)
    return exp_scores / jnp.sum(exp_scores, axis=3, keepdims=True)


def attend(inputs):
    queries, keys_in, values_in = inputs
    utt_count, length, feat_width = queries.shape
    row_block = min(512, length)
    q_four = split_heads(queries)
    k_four = split_heads(keys_in)
    v_four = split_heads(values_in)

    def one_block(row_start):
        q_block = lax.dynamic_slice_in_dim(q_four, row_start, row_block, 1)
        prob_weights = softmax_rows(q_block, k_four).astype(jnp.bfloat16)
        return jnp.einsum(
            "bhqk,bkhd->bqhd", prob_weights, v_four, preferred_element_type=jnp.float32
        ).astype(jnp.bfloat16)

    starts = jnp.arange(length // row_block, dtype=jnp.int32) * row_block
    blocks_out = lax.map(one_block, starts)
    attended = jnp.moveaxis(blocks_out, 0, 1).reshape(utt_count, length, feat_width)
    return (attended, queries, keys_in, values_in)


def attend_back(queries, keys_in, values_in, grads_in):
    utt_count, length, feat_width = queries.shape
    row_block = min(512, length)
    factor = 1.0 / math.sqrt(HD)
    q_four = split_heads(queries)
    k_four = split_heads(keys_in)
    v_four = split_heads(values_in)
    g_four = split_heads(grads_in)

    def back_block(carried, row_start):
        key_acc, value_acc = carried
        q_block = lax.dynamic_slice_in_dim(q_four, row_start, row_block, 1)
        g_block = lax.dynamic_slice_in_dim(g_four, row_start, row_block, 1)
        prob_rows = softmax_rows(q_block, k_four)
        prob_weights = prob_rows.astype(jnp.bfloat16)
        grad_probs = jnp.einsum(
            "bqhd,bkhd->bhqk", g_block, v_four, preferred_element_type=jnp.float32
        )
        row_delta = jnp.sum(grad_probs * prob_rows, axis=3, keepdims=True)
        grad_scores = (prob_rows * (grad_probs - row_delta) * factor).astype(jnp.bfloat16)
        value_acc = value_acc + jnp.einsum(
            "bhqk,bqhd->bkhd", prob_weights, g_block, preferred_element_type=jnp.float32
        )
        key_acc = key_acc + jnp.einsum(
            "bhqk,bqhd->bkhd", grad_scores, q_block, preferred_element_type=jnp.float32
        )
        query_grad = jnp.einsum(
            "bhqk,bkhd->bqhd", grad_scores, k_four, preferred_element_type=jnp.float32
        ).astype(jnp.bfloat16)
        return ((key_acc, value_acc), query_grad)

    zero_four = jnp.zeros(k_four.shape, jnp.float32)
    starts = jnp.arange(length // row_block, dtype=jnp.int32) * row_block
    (key_acc, value_acc), query_blocks = lax.scan(back_block, (zero_four, zero_four), starts)
    grad_queries = jnp.moveaxis(query_blocks, 0, 1).reshape(utt_count, length, feat_width)
    grad_keys = key_acc.astype(jnp.bfloat16).reshape(utt_count, length, feat_width)
    grad_values = value_acc.astype(jnp.bfloat16).reshape(utt_count, length, feat_width)
    return (grad_queries, grad_keys, grad_values)


def body(query, key_proj, value, cotangent, out_weight):
    utt_count, frames, feat_width = query.shape
    attended_heads, q_heads, k_heads, v_heads = attend(
        (
            lax.all_to_all(query, "seq", split_axis=2, concat_axis=1, tiled=True),
            lax.all_to_all(key_proj, "seq", split_axis=2, concat_axis=1, tiled=True),
            lax.all_to_all(value, "seq", split_axis=2, concat_axis=1, tiled=True),
        )
    )
    attended = lax.all_to_all(attended_heads, "seq", split_axis=1, concat_axis=2, tiled=True)
    attended_rows = attended.reshape(utt_count * frames, feat_width)
    grad_rows = cotangent.reshape(utt_count * frames, feat_width)
    columns = attended_rows
    projected = jnp.dot(
        columns,
        lax.all_gather(out_weight, ("dp", "seq"), axis=0, tiled=True),
        preferred_element_type=jnp.float32,
    )
    grad_attended = lax.dot_general(
        grad_rows,
        lax.all_gather(out_weight, ("dp", "seq"), axis=0, tiled=True),
        (((1,), (1,)), ((), ())),
        preferred_element_type=jnp.float32,
    )
    grad_local = grad_attended.astype(jnp.bfloat16).reshape(utt_count, frames, feat_width)
    grad_heads = lax.all_to_all(grad_local, "seq", split_axis=2, concat_axis=1, tiled=True)
    grad_queries, grad_keys, grad_values = attend_back(q_heads, k_heads, v_heads, grad_heads)
    grad_query, grad_key, grad_value = (
        lax.all_to_all(grad_queries, "seq", split_axis=1, concat_axis=2, tiled=True),
        lax.all_to_all(grad_keys, "seq", split_axis=1, concat_axis=2, tiled=True),
        lax.all_to_all(grad_values, "seq", split_axis=1, concat_axis=2, tiled=True),
    )
    columns = attended_rows
    grad_weight = lax.psum_scatter(
        lax.dot_general(
            columns, grad_rows, (((0,), (0,)), ((), ())), preferred_element_type=jnp.float32
        ),
        ("dp", "seq"),
        scatter_dimension=0,
        tiled=True,
    )
    projected_out = projected.astype(jnp.bfloat16).reshape(utt_count, frames, feat_width)
    return (projected_out, grad_query, grad_key, grad_value, grad_weight)


def solution(mesh):
    placed = (
        P("dp", "seq", None),
        P("dp", "seq", None),
        P("dp", "seq", None),
        P("dp", "seq", None),
        P(("dp", "seq"), None),
    )
    return jax.shard_map(
        body,
        mesh=mesh,
        in_specs=placed,
        out_specs=(
            P("dp", "seq", None),
            P("dp", "seq", None),
            P("dp", "seq", None),
            P("dp", "seq", None),
            P(("dp", "seq"), None),
        ),
        check_vma=False,
    )
```

profile of v0, /device:TPU:39, one launch (start us, length us, event | category | flops | bytes accessed | tf_op | source)
XLA Modules:
  0.0 2078.6 jit_solution(4284577261181988865)
XLA Ops:
  47.6 14.9 all-to-all-start.1
  84.7 14.5 all-to-all-done.2
  100.0 21.6 %while.25 = (s32[]{:T(128)}, bf16[4,1,512,1,96]{2,4,3,1,0:T(8,128)(2,1)S(1)}, s32[4]{0:T(128)S(1)}, bf16[1,2048,1,96]{1,3,2,0:T(8,128)(2,1)S(1)}, bf16[1,2048,1,...) while((s32[]{:T(128)}, ...), condition=%wide.region_3.4_spmd, body=%wide.region_0.3_spmd.sunk | while | flops 412138496 | bytes 13576347 | solution.py:43
  140.2 305.8 %all-gather.3.cloned.1.call-done = bf16[256,6,1536]{2,1,0:T(8,128)(2,1)} async-done(((bf16[1,6,1536]{2,1,0:T(8,128)(2,1)}), bf16[256,6,1536]{2,1,0:T(8,128)(2,1)}) %all-gather.3.cloned.1.call-update) | async-done | bytes 4718608 | tf_op jit(solution)/shard_map/all_gather | solution.py:103
  496.0 65.3 %while.26 = (s32[]{:T(128)}, f32[1,2048,1,96]{1,3,2,0:T(8,128)}, f32[1,2048,1,96]{1,3,2,0:T(8,128)}, bf16[4,1,512,1,96]{2,4,3,1,0:T(8,128)(2,1)}, s32[4]{0:T(128...) while((s32[]{:T(128)}, f32[1,2048,1,96]{1,3,2,0:T(8,128)}, ...), condition=%wide.region_8.9_spmd.clone, body=%wide.region_4.8_spmd.clone.sunk | while | flops 1029487104 | bytes 58841344 | solution.py:81
  609.5 819.5 %fusion = f32[8,1536]{1,0:T(8,128)} fusion(f32[1536,1536]{1,0:T(8,128)} %fusion.40), kind=kCustom, calls=%all-reduce-scatter | all-reduce-scatter fusion | flops 3145729 | bytes 9486336
  1551.3 15.7 collective-permute-start.28
  1606.4 13.1 collective-permute-start.24
  1619.5 13.1 collective-permute-start.23
  1632.7 13.1 collective-permute-start.22
  1645.9 13.1 collective-permute-start.21
  1659.0 13.1 collective-permute-start.20
  1672.1 13.1 collective-permute-start.19
  1685.3 13.1 collective-permute-start.18
  1698.4 13.1 collective-permute-start.17
  1711.6 13.1 collective-permute-start.16
  1724.7 13.1 collective-permute-start.15
  1737.9 13.1 collective-permute-start.14
  1751.0 13.1 collective-permute-start.13
  1764.1 13.1 collective-permute-start.12
  1777.3 13.1 collective-permute-start.11
  1790.4 13.3 collective-permute-start.10
  1945.9 13.4 collective-permute-start
  1960.5 98.0 %concatenate = f32[518,1536]{1,0:T(8,128)} concatenate(f32[6,1536]{1,0:T(8,128)} %copy-done.12, f32[8,1536]{1,0:T(8,128)} %copy-done.9, f32[8,1536]{1,0:T(8,128)} %copy-done.10, f32[8,1536]{1,0:T(8,128)} %copy-done.11, f32[8,1536]{1,0:T(8,128)} %copy-done.13, f32[8,1536]{1,0:T(8,128)} %copy-done.14, f32[8,1536]{1,0:T(8,128)} %copy-done.15, f32[8,1536]{1,0:T(8,128)} %copy-done.16, ...), dimensions={0} | concatenate | bytes 6365184
  (357 shorter events, 568.3 us)
Async XLA Ops:
  7.2 438.8 %all-gather.3.cloned.1.call-start = ((), (), s32[]{:S(2)}) async-start(), calls=%async_computation.8 | async-start | bytes 6316032 | tf_op jit(solution)/shard_map/all_gather | solution.py:103
  135.9 332.7 %all-to-all-start.3 = ((bf16[16,2,6144]{2,1,0:T(2,128)(2,1)}), bf16[16,2,6144]{2,1,0:T(2,128)(2,1)S(1)}, u32[]{:S(2)}, u32[]{:S(2)}) async-start(bf16[16,2,6144]{2,1,0:T(2,128)(2,1)} %reshape.153), calls=%async_computation.3 | async-start | bytes 786432 | tf_op jit(solution)/shard_map/all_to_all | solution.py:97
  599.8 1218.1 %all-to-all-start.6 = ((bf16[16,2,6144]{2,1,0:T(2,128)(2,1)}), bf16[16,2,6144]{2,1,0:T(2,128)(2,1)S(1)}, u32[]{:S(2)}, u32[]{:S(2)}) async-start(bf16[16,2,6144]{2,1,0:T(2,128)(2,1)} %reshape.159), calls=%async_computation.6 | async-start | bytes 786432 | tf_op jit(solution)/shard_map/all_to_all | solution.py:117
  1551.3 68.3 %collective-permute-start.28 = (f32[8,1536]{1,0:T(8,128)}, f32[8,1536]{1,0:T(8,128)S(1)}, u32[]{:S(2)}, u32[]{:S(2)}) collective-permute-start(f32[8,1536]{1,0:T(8,128)} %fusion), channel_id=1, source_target_pairs={{0,29},{1,30},{2,31},{3,32},{4,33},{5,34},{6,35},{7,36},{8,37},{9,... | collective-permute-start | bytes 147464
  1566.9 65.7 %collective-permute-start.27 = (f32[8,1536]{1,0:T(8,128)}, f32[8,1536]{1,0:T(8,128)S(1)}, u32[]{:S(2)}, u32[]{:S(2)}) collective-permute-start(f32[8,1536]{1,0:T(8,128)} %fusion), channel_id=1, source_target_pairs={{0,28},{1,29},{2,30},{3,31},{4,32},{5,33},{6,34},{7,35},{8,36},{9,... | collective-permute-start | bytes 147464
  1580.1 65.7 %collective-permute-start.26 = (f32[8,1536]{1,0:T(8,128)}, f32[8,1536]{1,0:T(8,128)S(1)}, u32[]{:S(2)}, u32[]{:S(2)}) collective-permute-start(f32[8,1536]{1,0:T(8,128)} %fusion), channel_id=1, source_target_pairs={{0,27},{1,28},{2,29},{3,30},{4,31},{5,32},{6,33},{7,34},{8,35},{9,... | collective-permute-start | bytes 147464
  1593.2 65.7 %collective-permute-start.25 = (f32[8,1536]{1,0:T(8,128)}, f32[8,1536]{1,0:T(8,128)S(1)}, u32[]{:S(2)}, u32[]{:S(2)}) collective-permute-start(f32[8,1536]{1,0:T(8,128)} %fusion), channel_id=1, source_target_pairs={{0,26},{1,27},{2,28},{3,29},{4,30},{5,31},{6,32},{7,33},{8,34},{9,... | collective-permute-start | bytes 147464
  1606.4 65.7 %collective-permute-start.24 = (f32[8,1536]{1,0:T(8,128)}, f32[8,1536]{1,0:T(8,128)}, u32[]{:S(2)}, u32[]{:S(2)}) collective-permute-start(f32[8,1536]{1,0:T(8,128)} %fusion), channel_id=1, source_target_pairs={{0,25},{1,26},{2,27},{3,28},{4,29},{5,30},{6,31},{7,32},{8,33},{9,... | collective-permute-start | bytes 147464
  1619.5 65.7 %collective-permute-start.23 = (f32[8,1536]{1,0:T(8,128)}, f32[8,1536]{1,0:T(8,128)}, u32[]{:S(2)}, u32[]{:S(2)}) collective-permute-start(f32[8,1536]{1,0:T(8,128)} %fusion), channel_id=1, source_target_pairs={{0,24},{1,25},{2,26},{3,27},{4,28},{5,29},{6,30},{7,31},{8,32},{9,... | collective-permute-start | bytes 147464
  1632.7 65.7 %collective-permute-start.22 = (f32[8,1536]{1,0:T(8,128)}, f32[8,1536]{1,0:T(8,128)}, u32[]{:S(2)}, u32[]{:S(2)}) collective-permute-start(f32[8,1536]{1,0:T(8,128)} %fusion), channel_id=1, source_target_pairs={{0,23},{1,24},{2,25},{3,26},{4,27},{5,28},{6,29},{7,30},{8,31},{9,... | collective-permute-start | bytes 147464
  1645.9 65.7 %collective-permute-start.21 = (f32[8,1536]{1,0:T(8,128)}, f32[8,1536]{1,0:T(8,128)}, u32[]{:S(2)}, u32[]{:S(2)}) collective-permute-start(f32[8,1536]{1,0:T(8,128)} %fusion), channel_id=1, source_target_pairs={{0,22},{1,23},{2,24},{3,25},{4,26},{5,27},{6,28},{7,29},{8,30},{9,... | collective-permute-start | bytes 147464
  1659.0 65.7 %collective-permute-start.20 = (f32[8,1536]{1,0:T(8,128)}, f32[8,1536]{1,0:T(8,128)}, u32[]{:S(2)}, u32[]{:S(2)}) collective-permute-start(f32[8,1536]{1,0:T(8,128)} %fusion), channel_id=1, source_target_pairs={{0,21},{1,22},{2,23},{3,24},{4,25},{5,26},{6,27},{7,28},{8,29},{9,... | collective-permute-start | bytes 147464
  1672.1 65.7 %collective-permute-start.19 = (f32[8,1536]{1,0:T(8,128)}, f32[8,1536]{1,0:T(8,128)}, u32[]{:S(2)}, u32[]{:S(2)}) collective-permute-start(f32[8,1536]{1,0:T(8,128)} %fusion), channel_id=1, source_target_pairs={{0,20},{1,21},{2,22},{3,23},{4,24},{5,25},{6,26},{7,27},{8,28},{9,... | collective-permute-start | bytes 147464
  1685.3 65.7 %collective-permute-start.18 = (f32[8,1536]{1,0:T(8,128)}, f32[8,1536]{1,0:T(8,128)}, u32[]{:S(2)}, u32[]{:S(2)}) collective-permute-start(f32[8,1536]{1,0:T(8,128)} %fusion), channel_id=1, source_target_pairs={{0,19},{1,20},{2,21},{3,22},{4,23},{5,24},{6,25},{7,26},{8,27},{9,... | collective-permute-start | bytes 147464
  1698.4 65.7 %collective-permute-start.17 = (f32[8,1536]{1,0:T(8,128)}, f32[8,1536]{1,0:T(8,128)}, u32[]{:S(2)}, u32[]{:S(2)}) collective-permute-start(f32[8,1536]{1,0:T(8,128)} %fusion), channel_id=1, source_target_pairs={{0,18},{1,19},{2,20},{3,21},{4,22},{5,23},{6,24},{7,25},{8,26},{9,... | collective-permute-start | bytes 147464
  1711.6 65.7 %collective-permute-start.16 = (f32[8,1536]{1,0:T(8,128)}, f32[8,1536]{1,0:T(8,128)}, u32[]{:S(2)}, u32[]{:S(2)}) collective-permute-start(f32[8,1536]{1,0:T(8,128)} %fusion), channel_id=1, source_target_pairs={{0,17},{1,18},{2,19},{3,20},{4,21},{5,22},{6,23},{7,24},{8,25},{9,... | collective-permute-start | bytes 147464
  1724.7 65.7 %collective-permute-start.15 = (f32[8,1536]{1,0:T(8,128)}, f32[8,1536]{1,0:T(8,128)}, u32[]{:S(2)}, u32[]{:S(2)}) collective-permute-start(f32[8,1536]{1,0:T(8,128)} %fusion), channel_id=1, source_target_pairs={{0,16},{1,17},{2,18},{3,19},{4,20},{5,21},{6,22},{7,23},{8,24},{9,... | collective-permute-start | bytes 147464
  1737.9 89.9 %collective-permute-start.14 = (f32[8,1536]{1,0:T(8,128)}, f32[8,1536]{1,0:T(8,128)}, u32[]{:S(2)}, u32[]{:S(2)}) collective-permute-start(f32[8,1536]{1,0:T(8,128)} %fusion), channel_id=1, source_target_pairs={{0,15},{1,16},{2,17},{3,18},{4,19},{5,20},{6,21},{7,22},{8,23},{9,... | collective-permute-start | bytes 147464
  1751.0 89.7 %collective-permute-start.13 = (f32[8,1536]{1,0:T(8,128)}, f32[8,1536]{1,0:T(8,128)}, u32[]{:S(2)}, u32[]{:S(2)}) collective-permute-start(f32[8,1536]{1,0:T(8,128)} %fusion), channel_id=1, source_target_pairs={{0,14},{1,15},{2,16},{3,17},{4,18},{5,19},{6,20},{7,21},{8,22},{9,... | collective-permute-start | bytes 147464
  1764.1 89.7 %collective-permute-start.12 = (f32[8,1536]{1,0:T(8,128)}, f32[8,1536]{1,0:T(8,128)}, u32[]{:S(2)}, u32[]{:S(2)}) collective-permute-start(f32[8,1536]{1,0:T(8,128)} %fusion), channel_id=1, source_target_pairs={{0,13},{1,14},{2,15},{3,16},{4,17},{5,18},{6,19},{7,20},{8,21},{9,... | collective-permute-start | bytes 147464
  1777.3 89.7 %collective-permute-start.11 = (f32[8,1536]{1,0:T(8,128)}, f32[8,1536]{1,0:T(8,128)}, u32[]{:S(2)}, u32[]{:S(2)}) collective-permute-start(f32[8,1536]{1,0:T(8,128)} %fusion), channel_id=1, source_target_pairs={{0,12},{1,13},{2,14},{3,15},{4,16},{5,17},{6,18},{7,19},{8,20},{9,... | collective-permute-start | bytes 147464
  1790.4 89.7 %collective-permute-start.10 = (f32[8,1536]{1,0:T(8,128)}, f32[8,1536]{1,0:T(8,128)}, u32[]{:S(2)}, u32[]{:S(2)}) collective-permute-start(f32[8,1536]{1,0:T(8,128)} %fusion), channel_id=1, source_target_pairs={{0,11},{1,12},{2,13},{3,14},{4,15},{5,16},{6,17},{7,18},{8,19},{9,... | collective-permute-start | bytes 147464
  1818.0 251.0 %all-to-all-start.7 = ((bf16[16,2,6144]{2,1,0:T(2,128)(2,1)}), bf16[16,2,6144]{2,1,0:T(2,128)(2,1)S(1)}, u32[]{:S(2)}, u32[]{:S(2)}) async-start(bf16[16,2,6144]{2,1,0:T(2,128)(2,1)} %reshape.161), calls=%async_computation.7 | async-start | bytes 786432 | tf_op jit(solution)/shard_map/all_to_all | solution.py:118
  1893.3 65.9 %collective-permute-start.4 = (f32[8,1536]{1,0:T(8,128)}, f32[8,1536]{1,0:T(8,128)S(1)}, u32[]{:S(2)}, u32[]{:S(2)}) collective-permute-start(f32[8,1536]{1,0:T(8,128)} %fusion), channel_id=1, source_target_pairs={{0,5},{1,6},{2,7},{3,8},{4,9},{5,10},{6,11},{7,12},{8,13},{9,14},{... | collective-permute-start | bytes 147464
  (103 other events, 12843.4 us)
Sparse Core Ops, SparseCore 0:
  9.9 436.0 all-gather.2
where the time goes:
time: 2100 us; the launch traced here: 2080 us
  blocking collectives  820 us (39%)
  starting transfers between devices  543 us (26%)
  waiting for transfers between devices  377 us (18%)
  local copies, waits for them, and re-layouts  147 us (7%)
  other arithmetic  93.4 us (4%)
  matrix products  67.2 us (3%)
    unnamed x1, blocking collectives  820 us
    unnamed x64, starting transfers between devices  474 us
    all_gather x1, waiting for transfers between devices, body(): lax.all_gather(out_weight, ('dp', 'seq'), axis=0, tiled=True)  306 us
    unnamed x127, local copies, waits for them, and re-layouts  131 us
    unnamed x10, other arithmetic  80.7 us
  transfers between devices with their start and end apart: 73, of which 15 were waited for; matrix products, arithmetic and copies ran while one was open for 50% of the time, Pallas kernels for 0%

commit v1 on v0

v1 whole, which is shorter than its diff:
```python
import functools
import math

import jax
import jax.numpy as jnp
from jax import lax
from jax.experimental import pallas as pl
from jax.experimental.pallas import tpu as pltpu
from jax.sharding import Mesh
from jax.sharding import PartitionSpec as P

HD = 96
FACTOR = 1.0 / math.sqrt(HD)
LOG2E = math.log2(math.e)
C2 = FACTOR * LOG2E
F32 = jnp.float32
BF16 = jnp.bfloat16
NB = 8
FB = 128
QB = 2
PAIR = 2 * HD
ALL = ("zl", "x", "zh", "y", "c")
YC = ("y", "c")
G32 = ("zl", "x", "zh")


def vmem_specs(count):
    return [pl.BlockSpec(memory_space=pltpu.VMEM) for _ in range(count)]


def call(kernel, ins, outs, scratch=(), flops=0, name=None):
    nbytes = sum(a.size * a.dtype.itemsize for a in list(ins) + list(outs))
    return pl.pallas_call(
        kernel,
        out_shape=tuple(outs),
        in_specs=vmem_specs(len(ins)),
        out_specs=tuple(vmem_specs(len(outs))),
        scratch_shapes=list(scratch),
        cost_estimate=pl.CostEstimate(flops=flops, bytes_accessed=nbytes, transcendentals=0),
        compiler_params=pltpu.CompilerParams(vmem_limit_bytes=56 * 2**20),
        name=name,
    )(*ins)


def shape(dims, dtype):
    return jax.ShapeDtypeStruct(dims, dtype)


def nn(a, b):
    return jnp.dot(a, b, preferred_element_type=F32)


def heads_of(head, offset=0):
    return slice(offset + head * HD, offset + (head + 1) * HD)


def cols(ref, step, rows):
    return jnp.concatenate([ref[step * QB + t, rows, :] for t in range(QB)], axis=1)


def put_cols(ref, step, rows, value):
    for t in range(QB):
        ref[step * QB + t, rows, :] = value[:, t * FB : (t + 1) * FB].astype(ref.dtype)


def rows_from(ref, rows, out):
    for b in range(NB):
        out[b * FB : (b + 1) * FB, :] = ref[b, rows, :].T


def wide_from(ref, rows, out):
    for b in range(NB):
        out[:, b * FB : (b + 1) * FB] = ref[b, rows, :]


def prep_kernel(count, *refs):
    out = refs[count]
    for n in range(count):
        for b in range(NB):
            out[b, n * PAIR : (n + 1) * PAIR, :] = refs[n][:, b * PAIR : (b + 1) * PAIR].T


def prep(*arrays):
    count = len(arrays)
    return call(
        functools.partial(prep_kernel, count),
        arrays,
        [shape((NB, count * PAIR, FB), BF16)],
        name="prep",
    )[0]


def fwd_kernel(second, *refs):
    if second:
        q, kv, st_in, acc_in, att, acc_out, st_out, k_s, vt_s = refs
    else:
        q, kv, acc_out, st_out, k_s, vt_s = refs
    st_out[...] = jnp.zeros_like(st_out)
    for head in range(2):
        rows = heads_of(head)
        rows_from(kv, rows, k_s)
        wide_from(kv, heads_of(head, PAIR), vt_s)

        def step(i, carry, rows=rows, head=head):
            scores = nn(k_s[...], cols(q, i, rows))
            top = jnp.max(scores, axis=0, keepdims=True) * C2
            if second:
                top_old = cols(st_in, i, slice(head, head + 1))
                top = jnp.maximum(top, top_old)
            probs = jnp.exp2(scores * C2 - top)
            total = jnp.sum(probs, axis=0, keepdims=True)
            acc = nn(vt_s[...], probs.astype(BF16))
            if second:
                alpha = jnp.exp2(top_old - top)
                total = total + alpha * cols(st_in, i, slice(2 + head, 3 + head))
                acc = acc + alpha * cols(acc_in, i, rows)
                acc = acc / total
                put_cols(att, i, rows, acc)
                put_cols(st_out, i, slice(head, head + 1), top + jnp.log2(total))
            else:
                put_cols(st_out, i, slice(head, head + 1), top)
                put_cols(st_out, i, slice(2 + head, 3 + head), total)
            put_cols(acc_out, i, rows, acc)
            return carry

        lax.fori_loop(0, NB // QB, step, 0)


def forward(q, kv, state=None):
    second = state is not None
    outs = [shape((NB, PAIR, FB), F32), shape((NB, 8, FB), F32)]
    if second:
        outs = [shape((NB, PAIR, FB), BF16)] + outs
    ins = [q, kv] + (list(state) if second else [])
    return call(
        functools.partial(fwd_kernel, second),
        ins,
        outs,
        [pltpu.VMEM((NB * FB, HD), BF16), pltpu.VMEM((HD, NB * FB), BF16)],
        flops=4 * 2 * 1024 * 1024 * 256,
        name="fwd_rem" if second else "fwd_own",
    )


def grad_kernel(w32, cot, w_out, g_out, w_s):
    for n in range(32):
        w_s[n * 6 : (n + 1) * 6, :] = w32[n].astype(F32)
    w_pair = w_s[...].astype(BF16)
    w_out[...] = w_pair
    for b in range(NB):
        g_out[b] = lax.dot_general(
            w_pair, cot[b * FB : (b + 1) * FB, :], (((1,), (1,)), ((), ())), preferred_element_type=F32
        ).astype(BF16)


def grad_attended(w32, cot):
    return call(
        grad_kernel,
        [w32, cot],
        [shape((PAIR, 1536), BF16), shape((NB, PAIR, FB), BF16)],
        [pltpu.VMEM((PAIR, 1536), F32)],
        flops=2 * 192 * 1536 * 1024,
        name="grad_att",
    )


def delta_kernel(g, acc, st_in, st_out):
    for b in range(NB):
        st_out[b] = st_in[b]
        for head in range(2):
            rows = heads_of(head)
            st_out[b, 2 + head : 3 + head, :] = jnp.sum(
                g[b, rows, :].astype(F32) * acc[b, rows, :], axis=0, keepdims=True
            )


def deltas(g, acc, stats):
    return call(delta_kernel, [g, acc, stats], [shape((NB, 8, FB), F32)], name="delta")[0]


def bwd_kernel(need_q, need_k, first, last, *refs):
    refs = list(refs)
    q, g, st, kv = refs[:4]
    del refs[:4]
    dq_in = dkv_in = None
    if need_q and not first:
        dq_in = refs.pop(0)
    if need_k and not first:
        dk_in, dv_in = refs.pop(0), refs.pop(0)
    dq = refs.pop(0) if need_q else None
    if need_k:
        if last:
            dkv = refs.pop(0)
        else:
            dk_out, dv_out = refs.pop(0), refs.pop(0)
    k_s, v_s = refs.pop(0), refs.pop(0)
    if need_q:
        kt_s = refs.pop(0)
    if need_k:
        q_s, g_s, dk_s, dv_s = refs
    for head in range(2):
        rows = heads_of(head)
        rows_from(kv, rows, k_s)
        rows_from(kv, heads_of(head, PAIR), v_s)
        if need_q:
            wide_from(kv, rows, kt_s)
        if need_k:
            rows_from(q, rows, q_s)
            rows_from(g, rows, g_s)
            if first:
                dk_s[...] = jnp.zeros_like(dk_s)
                dv_s[...] = jnp.zeros_like(dv_s)
            else:
                dk_s[...] = dk_in[head]
                dv_s[...] = dv_in[head]

        def step(i, carry, rows=rows, head=head):
            lse = cols(st, i, slice(head, head + 1))
            delta = cols(st, i, slice(2 + head, 3 + head))
            scores = nn(k_s[...], cols(q, i, rows))
            probs = jnp.exp2(scores * C2 - lse)
            gprobs = nn(v_s[...], cols(g, i, rows))
            ds = (probs * (gprobs - delta)).astype(BF16)
            if need_q:
                acc = nn(kt_s[...], ds)
                if dq_in is not None:
                    acc = acc + cols(dq_in, i, rows)
                if last:
                    acc = acc * FACTOR
                put_cols(dq, i, rows, acc)
            if need_k:
                at = pl.ds(pl.multiple_of(i * (QB * FB), QB * FB), QB * FB)
                dv_s[...] += nn(probs.astype(BF16), g_s[at, :])
                dk_s[...] += nn(ds, q_s[at, :])
            return carry

        lax.fori_loop(0, NB // QB, step, 0)
        if need_k:
            if last:
                for b in range(NB):
                    part = slice(b * FB, (b + 1) * FB)
                    dkv[b, rows, :] = (dk_s[part, :] * FACTOR).T.astype(BF16)
                    dkv[b, heads_of(head, PAIR), :] = dv_s[part, :].T.astype(BF16)
            else:
                dk_out[head] = dk_s[...]
                dv_out[head] = dv_s[...]


def backward(q, g, stats, kv, dq=None, dkv=None, need_q=False, need_k=False, first=False, last=False, name=None):
    ins = [q, g, stats, kv]
    if dq is not None:
        ins.append(dq)
    if dkv is not None:
        ins += list(dkv)
    outs = []
    if need_q:
        outs.append(shape((NB, PAIR, FB), BF16 if last else F32))
    if need_k:
        if last:
            outs.append(shape((NB, 2 * PAIR, FB), BF16))
        else:
            outs += [shape((2, NB * FB, HD), F32)] * 2
    tall = pltpu.VMEM((NB * FB, HD), BF16)
    scratch = [tall, tall]
    if need_q:
        scratch.append(pltpu.VMEM((HD, NB * FB), BF16))
    if need_k:
        scratch += [tall, tall, pltpu.VMEM((NB * FB, HD), F32), pltpu.VMEM((NB * FB, HD), F32)]
    products = 2 + need_q + 2 * need_k
    return call(
        functools.partial(bwd_kernel, need_q, need_k, first, last),
        ins,
        outs,
        scratch,
        flops=products * 2 * 2 * 1024 * 1024 * 256,
        name=name,
    )


def weight_kernel(att, cot, out, w_s):
    acc = jnp.zeros((PAIR, 1536), F32)
    for b in range(NB):
        acc = acc + nn(att[b], cot[b * FB : (b + 1) * FB, :])
    w_s[...] = acc
    for n in range(32):
        out[n] = w_s[n * 6 : (n + 1) * 6, :].astype(BF16)


def weight_part(att, cot):
    return call(
        weight_kernel,
        [att, cot],
        [shape((32, 6, 1536), BF16)],
        [pltpu.VMEM((PAIR, 1536), F32)],
        flops=2 * 192 * 1536 * 1024,
        name="grad_w",
    )[0]


def back_kernel(count, src, *outs):
    for n in range(count):
        for b in range(NB):
            outs[n][:, b * PAIR : (b + 1) * PAIR] = src[b, n * PAIR : (n + 1) * PAIR, :].T


def back(src):
    count = src.shape[1] // PAIR
    return call(
        functools.partial(back_kernel, count), [src], [shape((FB, 1536), BF16)] * count, name="back"
    )


def weight_pairs():
    pairs = []
    for a in range(8):
        for n in range(32):
            b, s = divmod(n, 16)
            pairs.append(((2 * a + b) * 16 + s, n * 8 + a))
    return pairs


def body(query, key_proj, value, cotangent, out_weight):
    flip = [(0, 1), (1, 0)]
    a2a = functools.partial(lax.all_to_all, split_axis=0, concat_axis=0, tiled=True)
    swap = lambda x: lax.ppermute(x, "zh", flip)

    kv = a2a(prep(key_proj[0], value[0]), YC)
    q = a2a(prep(query[0]), YC)
    w_mine = lax.ppermute(out_weight, ALL, weight_pairs())
    w32 = a2a(jnp.broadcast_to(w_mine[None], (32, 6, 1536)), G32)
    cot = lax.all_gather(cotangent[0], YC, axis=0, tiled=True)
    kv_far = swap(kv)
    q_far = swap(q)

    state = forward(q, kv)
    w_pair, g = grad_attended(w32, cot)
    g_far = swap(g)
    w_full = lax.all_gather(w_pair, YC, axis=0, tiled=True)
    att, acc, stats = forward(q, kv_far, state=(state[1], state[0]))
    att_rows = a2a(att, YC).reshape(1536, FB)
    stats = deltas(g, acc, stats)
    stats_far = swap(stats)
    dq, dk, dv = backward(q, g, stats, kv, need_q=True, need_k=True, first=True, name="bwd_own")
    (dq,) = backward(q, g, stats, kv_far, dq=dq, need_q=True, last=True, name="bwd_q")
    dq_rows = a2a(dq, YC)
    (dkv,) = backward(q_far, g_far, stats_far, kv, dkv=(dk, dv), need_k=True, last=True, name="bwd_k")
    dkv_rows = a2a(dkv, YC)

    parts = a2a(weight_part(att, cot), G32)
    grad_weight = jnp.sum(parts.astype(F32), axis=0)
    grad_weight = lax.ppermute(grad_weight, ALL, [(d, s) for s, d in weight_pairs()])

    projected = lax.dot_general(
        att_rows, w_full, (((0,), (0,)), ((), ())), preferred_element_type=F32
    ).astype(BF16)
    (grad_query,) = back(dq_rows)
    grad_key, grad_value = back(dkv_rows)
    return (projected[None], grad_query[None], grad_key[None], grad_value[None], grad_weight)


def solution(mesh):
    fine = Mesh(mesh.devices.reshape(4, 4, 2, 4, 2), ALL)
    rows = P(("zl", "x"), ("zh", "y", "c"), None)
    weight = P(ALL, None)
    return jax.shard_map(
        body,
        mesh=fine,
        in_specs=(rows, rows, rows, rows, weight),
        out_specs=(rows, rows, rows, rows, weight),
        check_vma=False,
    )
```

time: 2100 us -> 262 us (0.12)
  blocking collectives: 820 us -> 108 us
  starting transfers between devices: 543 us -> 37 us
  waiting for transfers between devices: 377 us -> 25.5 us
  local copies, waits for them, and re-layouts: 147 us -> 2.4 us
  other arithmetic: 93.4 us -> 0.17 us
  Pallas kernels: 0 us -> 66.5 us
  matrix products: 67.2 us -> 3.89 us
    unnamed x1 -> x0, blocking collectives: 820 us -> none
    unnamed x64 -> x0, starting transfers between devices: 474 us -> none
    all_gather x1 -> x2, waiting for transfers between devices: 306 us -> 0.01 us  [the longest x1 0.01 us: body(): cot = lax.all_gather(cotangent[0], YC, axis=0, tiled=True)]
    unnamed x127 -> x19, local copies, waits for them, and re-layouts: 131 us -> 2.35 us
    all_to_all x0 -> x4, blocking collectives: none -> 108 us  [the longest x1 38.1 us: body(): parts = a2a(weight_part(att, cot), G32)]
    unnamed x10 -> x0, other arithmetic: 80.7 us -> none
    pallas_call x0 -> x12, Pallas kernels: none -> 66.5 us  [call(): pl.pallas_call(kernel, out_shape=tuple(outs), in_specs=vmem_specs(len(ins...]
    dot_general x31 -> x1, matrix products: 67.2 us -> 3.89 us  [body(): lax.dot_general(att_rows, w_full, (((0,), (0,)), ((), ())), preferred_ele...]
  transfers between devices with their start and end apart: 73 -> 11, of which waited for: 15 -> 4; matrix products, arithmetic and copies ran while one was open for 50% -> 0% of each run, Pallas kernels for 0% -> 24%
where the time goes in v1:
time: 262 us; the launch traced here: 257 us
  blocking collectives  108 us (41%)
  Pallas kernels  66.5 us (25%)
  starting transfers between devices  37 us (14%)
  waiting for transfers between devices  25.5 us (10%)
  between operations  14.1 us (5%)
  matrix products  3.89 us (1%)
    pallas_call x12, Pallas kernels, call(): pl.pallas_call(kernel, out_shape=tuple(outs), in_specs=vmem_specs(len(ins...  66.5 us
    all_to_all x1, blocking collectives, body(): parts = a2a(weight_part(att, cot), G32)  38.1 us
    all_to_all x1, blocking collectives, body(): w32 = a2a(jnp.broadcast_to(w_mine[None], (32, 6, 1536)), G32)  28.8 us
    all_to_all x1, blocking collectives, body(): kv = a2a(prep(key_proj[0], value[0]), YC)  26.7 us
    all_to_all x1, blocking collectives, body(): q = a2a(prep(query[0]), YC)  14.3 us
    ppermute x4, starting transfers between devices, body(): swap = lambda x: lax.ppermute(x, 'zh', flip)  9.98 us
    ppermute x4, waiting for transfers between devices, body(): swap = lambda x: lax.ppermute(x, 'zh', flip)  9.65 us
    ppermute x1, starting transfers between devices, body(): w_mine = lax.ppermute(out_weight, ALL, weight_pairs())  8.4 us
  transfers between devices with their start and end apart: 11, of which 4 were waited for; matrix products, arithmetic and copies ran while one was open for 0% of the time, Pallas kernels for 24%

profile of v1, /device:TPU:39, one launch (start us, length us, event | category | flops | bytes accessed | tf_op | source)
XLA Modules:
  0.0 257.5 jit_solution(10897518371111631278)
XLA Ops:
  7.9 8.4 %collective-permute-start.1 = (bf16[6,1536]{1,0:T(8,128)(2,1)}, bf16[6,1536]{1,0:T(8,128)(2,1)S(1)}, u32[]{:S(2)}, u32[]{:S(2)}) collective-permute-start(bf16[6,1536]{1,0:T(8,128)(2,1)} %param.9), channel_id=1, source_target_pairs={{0,0},{1,8},{2,16},{3,24},{4,32},{5,40},{6,48},{7,56},{8,64},{9,72... | collective-permute-start | bytes 55304 | tf_op jit(solution)/shard_map/ppermute | solution.py:329
  16.4 4.3 %collective-permute-done.1 = bf16[6,1536]{1,0:T(8,128)(2,1)S(1)} collective-permute-done((bf16[6,1536]{1,0:T(8,128)(2,1)}, bf16[6,1536]{1,0:T(8,128)(2,1)S(1)}, u32[]{:S(2)}, u32[]{:S(2)}) %collective-permute-start.1) | collective-permute-done | bytes 18464 | tf_op jit(solution)/shard_map/ppermute | solution.py:329
  20.7 28.8 %all_to_all.35.w32 = bf16[32,6,1536]{2,1,0:T(8,128)(2,1)} all-to-all(bf16[32,6,1536]{2,1,0:T(8,128)(2,1)S(1)} %broadcast_in_dim.18), channel_id=1, replica_groups=mesh['zl'=4,'x'=4,'zh'=2,'y'=4,'c'=2] {'zl','x','zh'}, dimensions={0} | all-to-all | bytes 1179648 | tf_op jit(solution)/shard_map/all_to_all | solution.py:330
  49.5 4.4 %grad_att.1 = (bf16[192,1536]{1,0:T(8,128)(2,1)}, bf16[8,192,128]{2,1,0:T(8,128)(2,1)}) custom-call(bf16[32,6,1536]{2,1,0:T(8,128)(2,1)} %all_to_all.35.w32, bf16[1024,1536]{1,0:T(8,128)(2,1)} %bitcast.12), custom_call_target="tpu_custom_call" | custom-call | flops 603979776 | bytes 4718592 | tf_op jit(solution)/shard_map/grad_att/pallas_call | solution.py:33
  53.9 2.8 %prep.3 = bf16[8,384,128]{2,1,0:T(8,128)(2,1)} custom-call(bf16[128,1536]{1,0:T(8,128)(2,1)} %bitcast.17, bf16[128,1536]{1,0:T(8,128)(2,1)} %bitcast.18), custom_call_target="tpu_custom_call" | custom-call | bytes 1572864 | tf_op jit(solution)/shard_map/prep/pallas_call | solution.py:33
  56.8 26.7 %all_to_all.36.refs_1_.refs_3_ = bf16[8,384,128]{2,1,0:T(8,128)(2,1)S(1)} all-to-all(bf16[8,384,128]{2,1,0:T(8,128)(2,1)} %prep.3), channel_id=1, replica_groups=mesh['zl'=4,'x'=4,'zh'=2,'y'=4,'c'=2] {'y','c'}, dimensions={0} | all-to-all | bytes 1572864 | tf_op jit(solution)/shard_map/all_to_all | solution.py:327
  85.8 14.3 %all_to_all.37.refs_0_ = bf16[8,192,128]{2,1,0:T(8,128)(2,1)S(1)} all-to-all(bf16[8,192,128]{2,1,0:T(8,128)(2,1)} %prep.2), channel_id=1, replica_groups=mesh['zl'=4,'x'=4,'zh'=2,'y'=4,'c'=2] {'y','c'}, dimensions={0} | all-to-all | bytes 786432 | tf_op jit(solution)/shard_map/all_to_all | solution.py:328
  100.1 4.6 %collective-permute-start.2 = (bf16[8,192,128]{2,1,0:T(8,128)(2,1)S(1)}, bf16[8,192,128]{2,1,0:T(8,128)(2,1)S(1)}, u32[]{:S(2)}, u32[]{:S(2)}) collective-permute-start(bf16[8,192,128]{2,1,0:T(8,128)(2,1)S(1)} %all_to_all.37.refs_0_), channel_id=1, source_target_pairs={{0,8},{8,0},{1,9},{9,1},{2,10},{10,2},{3,11},{11,3},{4,12},{12,4},... | collective-permute-start | bytes 1179656 | tf_op jit(solution)/shard_map/ppermute | solution.py:325
  104.7 8.7 %fwd_own.1 = (f32[8,192,128]{2,1,0:T(8,128)}, f32[8,8,128]{2,1,0:T(8,128)}) custom-call(bf16[8,192,128]{2,1,0:T(8,128)(2,1)} %copy-done.4, bf16[8,384,128]{2,1,0:T(8,128)(2,1)} %copy-done.2), custom_call_target="tpu_custom_call" | custom-call | flops 2147483648 | bytes 1998848 | tf_op jit(solution)/shard_map/fwd_own/pallas_call | solution.py:33
  113.4 9.6 %collective-permute-done.refs_1_.refs_3_ = bf16[8,384,128]{2,1,0:T(8,128)(2,1)S(1)} collective-permute-done((bf16[8,384,128]{2,1,0:T(8,128)(2,1)S(1)}, bf16[8,384,128]{2,1,0:T(8,128)(2,1)S(1)}, u32[]{:S(2)}, u32[]{:S(2)}) %collective-permute-start) | collective-permute-done | bytes 786464 | tf_op jit(solution)/shard_map/ppermute | solution.py:325
  123.9 9.0 %fwd_rem.1 = (bf16[8,192,128]{2,1,0:T(8,128)(2,1)}, f32[8,192,128]{2,1,0:T(8,128)}, f32[8,8,128]{2,1,0:T(8,128)}) custom-call(bf16[8,192,128]{2,1,0:T(8,128)(2,1)} %copy-done.4, bf16[8,384,128]{2,1,0:T(8,128)(2,1)} %copy-done.5, f32[8,8,128]{2,1,0:T(8,128)} %get-tuple-element.17.refs_2_, f32[8,192,128]{2,1,0:T(8,128)} %get-tuple-element.18.refs_3_), custom_call_target="tpu_custom_call" | custom-call | flops 2147483648 | bytes 3211264 | tf_op jit(solution)/shard_map/fwd_rem/pallas_call | solution.py:33
  135.0 5.2 %collective-permute-start.4 = (f32[8,8,128]{2,1,0:T(8,128)}, f32[8,8,128]{2,1,0:T(8,128)S(1)}, u32[]{:S(2)}, u32[]{:S(2)}) collective-permute-start(f32[8,8,128]{2,1,0:T(8,128)} %delta.1.refs_2_), channel_id=1, source_target_pairs={{0,8},{8,0},{1,9},{9,1},{2,10},{10,2},{3,11},{11,3},{4,12},{12,4},... | collective-permute-start | bytes 98312 | tf_op jit(solution)/shard_map/ppermute | solution.py:325
  140.2 11.0 %bwd_own.1 = (f32[8,192,128]{2,1,0:T(8,128)}, f32[2,1024,96]{2,1,0:T(8,128)}, f32[2,1024,96]{2,1,0:T(8,128)}) custom-call(bf16[8,192,128]{2,1,0:T(8,128)(2,1)} %copy-done.4, bf16[8,192,128]{2,1,0:T(8,128)(2,1)} %get-tuple-element.21.g.refs_1_, f32[8,8,128]{2,1,0:T(8,128)} %delta.1.refs_2_, bf16[8,384,128]{2,1,0:T(8,128)(2,1)} %copy-done.2), custom_call_target="tpu_custom_call" | custom-call | flops 5368709120 | bytes 3964928 | tf_op jit(solution)/shard_map/bwd_own/pallas_call | solution.py:33
  151.2 7.8 %bwd_q.1 = bf16[8,192,128]{2,1,0:T(8,128)(2,1)} custom-call(bf16[8,192,128]{2,1,0:T(8,128)(2,1)} %copy-done.4, bf16[8,192,128]{2,1,0:T(8,128)(2,1)} %get-tuple-element.21.g.refs_1_, f32[8,8,128]{2,1,0:T(8,128)} %delta.1.refs_2_, bf16[8,384,128]{2,1,0:T(8,128)(2,1)} %copy-done.5, f32[8,192,128]{2,1,0:T(8,128)} %get-tuple-element.24.refs_4_), custom_call_target="tpu_custom_call" | custom-call | flops 3221225472 | bytes 2785280 | tf_op jit(solution)/shard_map/bwd_q/pallas_call | solution.py:33
  159.1 4.6 %all-to-all-start.4 = ((bf16[8,192,128]{2,1,0:T(8,128)(2,1)}), bf16[8,192,128]{2,1,0:T(8,128)(2,1)S(1)}, u32[]{:S(2)}, u32[]{:S(2)}) async-start(bf16[8,192,128]{2,1,0:T(8,128)(2,1)} %bwd_q.1), calls=%async_computation.4 | async-start | bytes 786432 | tf_op jit(solution)/shard_map/all_to_all | solution.py:345
  164.6 9.6 %bwd_k.1 = bf16[8,384,128]{2,1,0:T(8,128)(2,1)} custom-call(bf16[8,192,128]{2,1,0:T(8,128)(2,1)} %copy-done.6, bf16[8,192,128]{2,1,0:T(8,128)(2,1)} %copy-done.7, f32[8,8,128]{2,1,0:T(8,128)} %copy-done.8, bf16[8,384,128]{2,1,0:T(8,128)(2,1)} %copy-done.2, f32[2,1024,96]{2,1,0:T(8,128)} %get-tuple-element.25.refs_4_, f32[2,1024,96]{2,1,0:T(8,128)} %get-tuple-element.26.refs_5_), custom_call_target="tpu_custom_call" | custom-call | flops 4294967296 | bytes 3964928 | tf_op jit(solution)/shard_map/bwd_k/pallas_call | solution.py:33
  174.1 4.8 %all-to-all-start.5 = ((bf16[8,384,128]{2,1,0:T(8,128)(2,1)}), bf16[8,384,128]{2,1,0:T(8,128)(2,1)S(1)}, u32[]{:S(2)}, u32[]{:S(2)}) async-start(bf16[8,384,128]{2,1,0:T(8,128)(2,1)} %bwd_k.1), calls=%async_computation.5 | async-start | bytes 1572864 | tf_op jit(solution)/shard_map/all_to_all | solution.py:347
  178.9 4.4 %grad_w.1 = bf16[32,6,1536]{2,1,0:T(8,128)(2,1)} custom-call(bf16[8,192,128]{2,1,0:T(8,128)(2,1)} %get-tuple-element.19.att, bf16[1024,1536]{1,0:T(8,128)(2,1)} %bitcast.13), custom_call_target="tpu_custom_call" | custom-call | flops 603979776 | bytes 4128768 | tf_op jit(solution)/shard_map/grad_w/pallas_call | solution.py:33
  183.3 7.9 %all-to-all-done.5.src = bf16[8,384,128]{2,1,0:T(8,128)(2,1)S(1)} async-done(((bf16[8,384,128]{2,1,0:T(8,128)(2,1)}), bf16[8,384,128]{2,1,0:T(8,128)(2,1)S(1)}, u32[]{:S(2)}, u32[]{:S(2)}) %all-to-all-start.5) | async-done | bytes 786464 | tf_op jit(solution)/shard_map/all_to_all | solution.py:347
  191.2 38.1 %all_to_all.38 = bf16[32,6,1536]{2,1,0:T(8,128)(2,1)S(1)} all-to-all(bf16[32,6,1536]{2,1,0:T(8,128)(2,1)} %grad_w.1), channel_id=1, replica_groups=mesh['zl'=4,'x'=4,'zh'=2,'y'=4,'c'=2] {'zl','x','zh'}, dimensions={0} | all-to-all | bytes 1179648 | tf_op jit(solution)/shard_map/all_to_all | solution.py:349
  229.4 5.2 %all-to-all-start.2 = ((bf16[8,192,128]{2,1,0:T(8,128)(2,1)}), bf16[8,192,128]{2,1,0:T(8,128)(2,1)S(1)}, u32[]{:S(2)}, u32[]{:S(2)}) async-start(bf16[8,192,128]{2,1,0:T(8,128)(2,1)} %get-tuple-element.19.att), calls=%async_computation.2 | async-start | bytes 786432 | tf_op jit(solution)/shard_map/all_to_all | solution.py:340
  234.7 4.0 %collective-permute-start.5 = (f32[6,1536]{1,0:T(8,128)S(1)}, f32[6,1536]{1,0:T(8,128)S(1)}, u32[]{:S(2)}, u32[]{:S(2)}) collective-permute-start(f32[6,1536]{1,0:T(8,128)S(1)} %convert_reduce_fusion), channel_id=1, source_target_pairs={{0,0},{8,1},{16,2},{24,3},{32,4},{40,5},{48,6},{56,7},{64,8},{72,9... | collective-permute-start | bytes 110600 | tf_op jit(solution)/shard_map/ppermute | solution.py:351
  243.2 2.9 %collective-permute-done.5 = f32[6,1536]{1,0:T(8,128)S(1)} collective-permute-done((f32[6,1536]{1,0:T(8,128)S(1)}, f32[6,1536]{1,0:T(8,128)S(1)}, u32[]{:S(2)}, u32[]{:S(2)}) %collective-permute-start.5) | collective-permute-done | bytes 36896 | tf_op jit(solution)/shard_map/ppermute | solution.py:351
  246.1 3.9 %fusion = bf16[1,128,1536]{2,1,0:T(8,128)(2,1)} fusion(bf16[1536,128]{1,0:T(8,128)(2,1)S(1)} %bitcast.14, bf16[1536,1536]{1,0:T(8,128)(2,1)} %all-gather.4.cloned.1.call-done), kind=kOutput, calls=%fused_computation.1 | convolution fusion | flops 604176384 | bytes 5505024 | tf_op jit(solution)/shard_map/dot_general | solution.py:353
  (38 shorter events, 12.3 us)
Async XLA Ops:
  7.2 42.3 %all-gather.6.cloned.1.call-start = ((), (), s32[]{:S(2)}) async-start(), calls=%async_computation.8 | async-start | bytes 3538944 | tf_op jit(solution)/shard_map/all_gather | solution.py:331
  7.9 238.2 %all-gather.4.cloned.1.call-start = ((), (), s32[]{:S(2)}) async-start(), calls=%async_computation.7 | async-start | bytes 5308416 | tf_op jit(solution)/shard_map/all_gather | solution.py:338
  7.9 12.7 %collective-permute-start.1 = (bf16[6,1536]{1,0:T(8,128)(2,1)}, bf16[6,1536]{1,0:T(8,128)(2,1)S(1)}, u32[]{:S(2)}, u32[]{:S(2)}) collective-permute-start(bf16[6,1536]{1,0:T(8,128)(2,1)} %param.9), channel_id=1, source_target_pairs={{0,0},{1,8},{2,16},{3,24},{4,32},{5,40},{6,48},{7,56},{8,64},{9,72... | collective-permute-start | bytes 55304 | tf_op jit(solution)/shard_map/ppermute | solution.py:329
  83.4 21.3 %copy-start.2 = (bf16[8,384,128]{2,1,0:T(8,128)(2,1)}, bf16[8,384,128]{2,1,0:T(8,128)(2,1)S(1)}, u32[]{:S(2)}) copy-start(bf16[8,384,128]{2,1,0:T(8,128)(2,1)S(1)} %all_to_all.36.refs_1_.refs_3_) | copy-start | bytes 2359300
  83.4 39.6 %collective-permute-start = (bf16[8,384,128]{2,1,0:T(8,128)(2,1)S(1)}, bf16[8,384,128]{2,1,0:T(8,128)(2,1)S(1)}, u32[]{:S(2)}, u32[]{:S(2)}) collective-permute-start(bf16[8,384,128]{2,1,0:T(8,128)(2,1)S(1)} %all_to_all.36.refs_1_.refs_3_), channel_id=1, source_target_pairs={{0,8},{8,0},{1,9},{9,1},{2,10},{10,2},{3,11},{11,3},{4,12},{12,4},... | collective-permute-start | bytes 2359304 | tf_op jit(solution)/shard_map/ppermute | solution.py:325
  100.1 4.6 %copy-start.4 = (bf16[8,192,128]{2,1,0:T(8,128)(2,1)}, bf16[8,192,128]{2,1,0:T(8,128)(2,1)S(1)}, u32[]{:S(2)}) copy-start(bf16[8,192,128]{2,1,0:T(8,128)(2,1)S(1)} %all_to_all.37.refs_0_) | copy-start | bytes 1179652
  100.1 63.6 %collective-permute-start.2 = (bf16[8,192,128]{2,1,0:T(8,128)(2,1)S(1)}, bf16[8,192,128]{2,1,0:T(8,128)(2,1)S(1)}, u32[]{:S(2)}, u32[]{:S(2)}) collective-permute-start(bf16[8,192,128]{2,1,0:T(8,128)(2,1)S(1)} %all_to_all.37.refs_0_), channel_id=1, source_target_pairs={{0,8},{8,0},{1,9},{9,1},{2,10},{10,2},{3,11},{11,3},{4,12},{12,4},... | collective-permute-start | bytes 1179656 | tf_op jit(solution)/shard_map/ppermute | solution.py:325
  113.4 19.5 %copy-start.3 = (bf16[8,192,128]{2,1,0:T(8,128)(2,1)S(1)}, bf16[8,192,128]{2,1,0:T(8,128)(2,1)}, u32[]{:S(2)}) copy-start(bf16[8,192,128]{2,1,0:T(8,128)(2,1)} %get-tuple-element.21.g.refs_1_) | copy-start | bytes 1179652
  123.0 0.9 copy-start.5
  132.9 30.8 %collective-permute-start.3 = (bf16[8,192,128]{2,1,0:T(8,128)(2,1)S(1)}, bf16[8,192,128]{2,1,0:T(8,128)(2,1)S(1)}, u32[]{:S(2)}, u32[]{:S(2)}) collective-permute-start(bf16[8,192,128]{2,1,0:T(8,128)(2,1)S(1)} %copy-done.3), channel_id=1, source_target_pairs={{0,8},{8,0},{1,9},{9,1},{2,10},{10,2},{3,11},{11,3},{4,12},{12,4},... | collective-permute-start | bytes 1179656 | tf_op jit(solution)/shard_map/ppermute | solution.py:325
  135.0 28.7 %collective-permute-start.4 = (f32[8,8,128]{2,1,0:T(8,128)}, f32[8,8,128]{2,1,0:T(8,128)S(1)}, u32[]{:S(2)}, u32[]{:S(2)}) collective-permute-start(f32[8,8,128]{2,1,0:T(8,128)} %delta.1.refs_2_), channel_id=1, source_target_pairs={{0,8},{8,0},{1,9},{9,1},{2,10},{10,2},{3,11},{11,3},{4,12},{12,4},... | collective-permute-start | bytes 98312 | tf_op jit(solution)/shard_map/ppermute | solution.py:325
  159.1 15.0 %all-to-all-start.4 = ((bf16[8,192,128]{2,1,0:T(8,128)(2,1)}), bf16[8,192,128]{2,1,0:T(8,128)(2,1)S(1)}, u32[]{:S(2)}, u32[]{:S(2)}) async-start(bf16[8,192,128]{2,1,0:T(8,128)(2,1)} %bwd_q.1), calls=%async_computation.4 | async-start | bytes 786432 | tf_op jit(solution)/shard_map/all_to_all | solution.py:345
  163.7 0.7 copy-start.6
  163.7 0.7 copy-start.8
  163.7 0.8 copy-start.7
  174.1 64.6 %copy-start.1 = (bf16[8,192,128]{2,1,0:T(8,128)(2,1)}, bf16[8,192,128]{2,1,0:T(8,128)(2,1)S(1)}, u32[]{:S(2)}) copy-start(bf16[8,192,128]{2,1,0:T(8,128)(2,1)S(1)} %all-to-all-done.4.src) | copy-start | bytes 1179652
  174.1 17.1 %all-to-all-start.5 = ((bf16[8,384,128]{2,1,0:T(8,128)(2,1)}), bf16[8,384,128]{2,1,0:T(8,128)(2,1)S(1)}, u32[]{:S(2)}, u32[]{:S(2)}) async-start(bf16[8,384,128]{2,1,0:T(8,128)(2,1)} %bwd_k.1), calls=%async_computation.5 | async-start | bytes 1572864 | tf_op jit(solution)/shard_map/all_to_all | solution.py:347
  191.2 49.5 %copy-start = (bf16[8,384,128]{2,1,0:T(8,128)(2,1)}, bf16[8,384,128]{2,1,0:T(8,128)(2,1)S(1)}, u32[]{:S(2)}) copy-start(bf16[8,384,128]{2,1,0:T(8,128)(2,1)S(1)} %all-to-all-done.5.src) | copy-start | bytes 2359300
  229.4 16.7 %all-to-all-start.2 = ((bf16[8,192,128]{2,1,0:T(8,128)(2,1)}), bf16[8,192,128]{2,1,0:T(8,128)(2,1)S(1)}, u32[]{:S(2)}, u32[]{:S(2)}) async-start(bf16[8,192,128]{2,1,0:T(8,128)(2,1)} %get-tuple-element.19.att), calls=%async_computation.2 | async-start | bytes 786432 | tf_op jit(solution)/shard_map/all_to_all | solution.py:340
  234.7 11.4 %collective-permute-start.5 = (f32[6,1536]{1,0:T(8,128)S(1)}, f32[6,1536]{1,0:T(8,128)S(1)}, u32[]{:S(2)}, u32[]{:S(2)}) collective-permute-start(f32[6,1536]{1,0:T(8,128)S(1)} %convert_reduce_fusion), channel_id=1, source_target_pairs={{0,0},{8,1},{16,2},{24,3},{32,4},{40,5},{48,6},{56,7},{64,8},{72,9... | collective-permute-start | bytes 110600 | tf_op jit(solution)/shard_map/ppermute | solution.py:351
Sparse Core Ops, SparseCore 0:
  9.8 33.2 all-gather.5
  54.0 44.4 all-gather.3

commit v2 on v0

v2 whole, which is shorter than its diff:
```python
import functools
import math

import jax
import jax.numpy as jnp
from jax import lax
from jax.experimental import pallas as pl
from jax.experimental.pallas import tpu as pltpu
from jax.sharding import Mesh
from jax.sharding import PartitionSpec as P

HD = 96
FACTOR = 1.0 / math.sqrt(HD)
LOG2E = math.log2(math.e)
C2 = FACTOR * LOG2E
F32 = jnp.float32
BF16 = jnp.bfloat16
NB = 16
HALF = 8
FB = 128
QB = 2
FRAMES = NB * FB
PAIR = 2 * HD
WIDTH = NB * HD
ALL = ("zl", "x", "zh", "y", "c")
SEQ = ("zh", "y", "c")
YC = ("y", "c")
Z8 = ("zl", "zh")


def call(kernel, ins, outs, scratch=(), side=False, us=1, name=None):
    vmem = pl.BlockSpec(memory_space=pltpu.VMEM)
    specs = [vmem for _ in ins]
    if side:
        ins = list(ins) + [lax.axis_index("zh").astype(jnp.int32).reshape(1)]
        specs.append(pl.BlockSpec(memory_space=pltpu.SMEM))
    return pl.pallas_call(
        kernel,
        out_shape=tuple(outs),
        in_specs=specs,
        out_specs=tuple(vmem for _ in outs),
        scratch_shapes=list(scratch),
        cost_estimate=pl.CostEstimate(flops=int(us * 1.1e9), bytes_accessed=1, transcendentals=0),
        compiler_params=pltpu.CompilerParams(vmem_limit_bytes=56 * 2**20),
        name=name,
    )(*ins)


def shape(dims, dtype):
    return jax.ShapeDtypeStruct(dims, dtype)


def nn(a, b):
    return jnp.dot(a, b, preferred_element_type=F32)


Q, K, V = (slice(n * HD, (n + 1) * HD) for n in range(3))
ANY = slice(0, HD)


def cols(ref, step, rows):
    return jnp.concatenate([ref[step * QB + t, rows, :] for t in range(QB)], axis=1)


def put_cols(ref, step, rows, value):
    for t in range(QB):
        ref[step * QB + t, rows, :] = value[:, t * FB : (t + 1) * FB].astype(ref.dtype)


def rows_from(ref, rows, out):
    for b in range(NB):
        out[b * FB : (b + 1) * FB, :] = ref[b, rows, :].T


def wide_from(ref, rows, out):
    for b in range(NB):
        out[:, b * FB : (b + 1) * FB] = ref[b, rows, :]


def prep_kernel(q, k, v, out):
    for n, ref in enumerate((q, k, v)):
        for part in range(4):
            four = ref[:, part * 4 * HD : (part + 1) * 4 * HD].T
            for h in range(4):
                out[part * 4 + h, n * HD : (n + 1) * HD, :] = four[h * HD : (h + 1) * HD, :]


def prep(q, k, v):
    return call(prep_kernel, [q, k, v], [shape((NB, 3 * HD, FB), BF16)], us=2.6, name="prep")[0]


def back_kernel(src, *outs):
    for n, out in enumerate(outs):
        for part in range(4):
            four = [src[part * 4 + h, n * HD : (n + 1) * HD, :] for h in range(4)]
            out[:, part * 4 * HD : (part + 1) * 4 * HD] = jnp.concatenate(four, axis=0).T


def back(src):
    return call(back_kernel, [src], [shape((FB, WIDTH), BF16)] * 3, us=2.4, name="back")


def fwd_kernel(qkv, side, keep, send, acc_out, lse_out, k_s, vt_s, att):
    rows_from(qkv, K, k_s)
    wide_from(qkv, V, vt_s)
    lse_out[...] = jnp.zeros_like(lse_out)

    def step(i, carry):
        scores = nn(k_s[...], cols(qkv, i, Q))
        top = jnp.max(scores, axis=0, keepdims=True) * C2
        probs = jnp.exp2(scores * C2 - top)
        total = jnp.sum(probs, axis=0, keepdims=True)
        acc = nn(vt_s[...], probs.astype(BF16)) / total
        put_cols(att, i, ANY, acc)
        put_cols(acc_out, i, ANY, acc)
        put_cols(lse_out, i, slice(0, 1), top + jnp.log2(total))
        return carry

    lax.fori_loop(0, NB // QB, step, 0)
    mine = side[0] * HALF
    for b in range(HALF):
        keep[b] = att[mine + b]
        send[b] = att[HALF - mine + b]


def forward(qkv):
    half = shape((HALF, HD, FB), BF16)
    return call(
        fwd_kernel,
        [qkv],
        [half, half, shape((NB, HD, FB), F32), shape((NB, 8, FB), F32)],
        [
            pltpu.VMEM((FRAMES, HD), BF16),
            pltpu.VMEM((HD, FRAMES), BF16),
            pltpu.VMEM((NB, HD, FB), BF16),
        ],
        side=True,
        us=12.4,
        name="fwd",
    )


def grad_kernel(w32, cot, att, side, keep, send, proj, w_s):
    for n in range(32):
        w_s[n * 6 : (n + 1) * 6, :] = w32[n].astype(F32)
    w_pair = w_s[...].astype(BF16)
    low = side[0] == 0
    for b in range(HALF):
        rows = slice(b * FB, (b + 1) * FB)
        both = lax.dot_general(
            w_pair, cot[rows, :], (((1,), (1,)), ((), ())), preferred_element_type=F32
        )
        keep[b] = jnp.where(low, both[:HD], both[HD:]).astype(BF16)
        send[b] = jnp.where(low, both[HD:], both[:HD]).astype(BF16)
        proj[rows, :] = nn(att[b].T, w_pair).astype(BF16)


def grad_attended(w32, cot, att_pair):
    half = shape((HALF, HD, FB), BF16)
    return call(
        grad_kernel,
        [w32, cot, att_pair],
        [half, half, shape((HALF * FB, WIDTH), BF16)],
        [pltpu.VMEM((PAIR, WIDTH), F32)],
        side=True,
        us=6.1,
        name="grad_att",
    )


def bwd_kernel(qkv, keep, recv, acc_in, lse_in, side, out, k_s, v_s, kt_s, q_s, g_s, gt_s, dk_s, dv_s):
    mine = side[0] * HALF
    for b in range(HALF):
        gt_s[mine + b] = keep[b]
        gt_s[HALF - mine + b] = recv[b]
    rows_from(qkv, K, k_s)
    rows_from(qkv, V, v_s)
    rows_from(qkv, Q, q_s)
    rows_from(gt_s, ANY, g_s)
    wide_from(qkv, K, kt_s)
    dk_s[...] = jnp.zeros_like(dk_s)
    dv_s[...] = jnp.zeros_like(dv_s)

    def step(i, carry):
        g = cols(gt_s, i, ANY)
        delta = jnp.sum(g.astype(F32) * cols(acc_in, i, ANY), axis=0, keepdims=True)
        scores = nn(k_s[...], cols(qkv, i, Q))
        probs = jnp.exp2(scores * C2 - cols(lse_in, i, slice(0, 1)))
        gprobs = nn(v_s[...], g)
        ds = (probs * (gprobs - delta)).astype(BF16)
        put_cols(out, i, Q, nn(kt_s[...], ds) * FACTOR)
        at = pl.ds(pl.multiple_of(i * (QB * FB), QB * FB), QB * FB)
        dv_s[...] += nn(probs.astype(BF16), g_s[at, :])
        dk_s[...] += nn(ds, q_s[at, :])
        return carry

    lax.fori_loop(0, NB // QB, step, 0)
    for b in range(NB):
        part = slice(b * FB, (b + 1) * FB)
        out[b, K, :] = (dk_s[part, :] * FACTOR).T.astype(BF16)
        out[b, V, :] = dv_s[part, :].T.astype(BF16)


def backward(qkv, keep, recv, acc, lse):
    tall = pltpu.VMEM((FRAMES, HD), BF16)
    total = pltpu.VMEM((FRAMES, HD), F32)
    return call(
        bwd_kernel,
        [qkv, keep, recv, acc, lse],
        [shape((NB, 3 * HD, FB), BF16)],
        [
            tall,
            tall,
            pltpu.VMEM((HD, FRAMES), BF16),
            tall,
            tall,
            pltpu.VMEM((NB, HD, FB), BF16),
            total,
            total,
        ],
        side=True,
        us=16.2,
        name="bwd",
    )[0]


def weight_kernel(keep, recv, cot, side, out, pair, w_s):
    low = side[0] == 0
    acc = jnp.zeros((PAIR, WIDTH), F32)
    for b in range(HALF):
        mine, other = keep[b], recv[b]
        both = jnp.concatenate([jnp.where(low, mine, other), jnp.where(low, other, mine)], axis=0)
        pair[b] = both
        acc = acc + nn(both, cot[b * FB : (b + 1) * FB, :])
    w_s[...] = acc
    for n in range(32):
        out[n] = w_s[n * 6 : (n + 1) * 6, :].astype(BF16)


def weight_part(keep, recv, cot):
    return call(
        weight_kernel,
        [keep, recv, cot],
        [shape((32, 6, WIDTH), BF16), shape((HALF, PAIR, FB), BF16)],
        [pltpu.VMEM((PAIR, WIDTH), F32)],
        side=True,
        us=4.4,
        name="grad_w",
    )


def weight_pairs():
    pairs = []
    for a in range(8):
        for n in range(32):
            b, s = divmod(n, 16)
            x, zl, zh = n // 8, n % 8 // 2, n % 2
            pairs.append(((a + 8 * b) * 16 + s, ((zl * 4 + x) * 2 + zh) * 8 + a))
    return pairs


def body(query, key_proj, value, cotangent, out_weight):
    flip = [(0, 1), (1, 0)]
    a2a = functools.partial(lax.all_to_all, split_axis=0, concat_axis=0, tiled=True)
    swap = lambda x: lax.ppermute(x, "zh", flip)
    after = lambda x, *others: lax.optimization_barrier((x, *others))[0]

    qkv = a2a(prep(query[0], key_proj[0], value[0]), SEQ)
    w_mine = lax.ppermute(after(out_weight, qkv), ALL, weight_pairs())
    cot = lax.all_gather(after(cotangent[0], qkv), YC, axis=0, tiled=True)
    att_keep, att_send, acc, lse = forward(qkv)
    att_recv = swap(att_send)
    w8 = a2a(after(jnp.broadcast_to(w_mine[None], (8, 6, WIDTH)), lse), Z8)
    w8 = after(w8, att_recv)
    w32 = a2a(jnp.broadcast_to(w8[None], (4, 8, 6, WIDTH)), "x").reshape(32, 6, WIDTH)
    part, att_pair = weight_part(att_keep, att_recv, cot)
    g_keep, g_send, proj = grad_attended(after(w32, part), cot, att_pair)
    parts = a2a(part.reshape(4, 8, 6, WIDTH), "x")
    parts = jnp.sum(parts.astype(F32), axis=0).astype(BF16)
    g_recv = swap(after(g_send, parts))
    projected = lax.psum_scatter(proj, YC, scatter_dimension=0, tiled=True)
    out = backward(qkv, g_keep, g_recv, acc, after(lse, parts))
    parts = a2a(parts, Z8)
    grads = a2a(after(out, parts), SEQ)

    grad_weight = jnp.sum(parts.astype(F32), axis=0)
    grad_weight = lax.ppermute(after(grad_weight, grads), ALL, [(d, s) for s, d in weight_pairs()])
    grad_query, grad_key, grad_value = back(grads)
    return (projected[None], grad_query[None], grad_key[None], grad_value[None], grad_weight)


def solution(mesh):
    fine = Mesh(mesh.devices.reshape(4, 4, 2, 4, 2), ALL)
    rows = P(("zl", "x"), ("zh", "y", "c"), None)
    weight = P(ALL, None)
    return jax.shard_map(
        body,
        mesh=fine,
        in_specs=(rows, rows, rows, rows, weight),
        out_specs=(rows, rows, rows, rows, weight),
        check_vma=False,
    )
```

time: 2100 us -> 219 us (0.10)
  blocking collectives: 820 us -> 68.7 us
  starting transfers between devices: 543 us -> 33.3 us
  waiting for transfers between devices: 377 us -> 50.5 us
  local copies, waits for them, and re-layouts: 147 us -> 5.23 us
  other arithmetic: 93.4 us -> 0.14 us
  matrix products: 67.2 us -> 0 us
  Pallas kernels: 0 us -> 44.2 us
    unnamed x1 -> x0, blocking collectives: 820 us -> none
    unnamed x64 -> x0, starting transfers between devices: 474 us -> none
    all_gather x1, waiting for transfers between devices: 306 us -> 0.01 us  [body(): cot = lax.all_gather(after(cotangent[0], qkv), YC, axis=0, tiled=True)]
    unnamed x127 -> x13, local copies, waits for them, and re-layouts: 131 us -> 2.42 us
    unnamed x10 -> x0, other arithmetic: 80.7 us -> none
    all_to_all x0 -> x3, blocking collectives: none -> 68.7 us  [the longest x1 45 us: body(): qkv = a2a(prep(query[0], key_proj[0], value[0]), SEQ)]
    dot_general x31 -> x0, matrix products: 67.2 us -> none  [the longest x4 17.7 us: back_block(): jnp.einsum('bhqk,bqhd->bkhd', prob_weights, g_block, preferred_element_ty...]
    all_to_all x8 -> x3, starting transfers between devices: 68.9 us -> 22.8 us  [the longest x1 13.8 us: body(): grads = a2a(after(out, parts), SEQ)]
  transfers between devices with their start and end apart: 73 -> 9, of which waited for: 15 -> 4; matrix products, arithmetic and copies ran while one was open for 50% -> 1% of each run, Pallas kernels for 0% -> 14%
where the time goes in v2:
time: 219 us; the launch traced here: 216 us
  blocking collectives  68.7 us (31%)
  waiting for transfers between devices  50.5 us (23%)
  Pallas kernels  44.2 us (20%)
  starting transfers between devices  33.3 us (15%)
  between operations  14.1 us (6%)
  local copies, waits for them, and re-layouts  5.23 us (2%)
    all_to_all x1, blocking collectives, body(): qkv = a2a(prep(query[0], key_proj[0], value[0]), SEQ)  45 us
    pallas_call x6, Pallas kernels, call(): pl.pallas_call(kernel, out_shape=tuple(outs), in_specs=specs, out_specs=t...  44.2 us
    all_to_all x1, waiting for transfers between devices, body(): grads = a2a(after(out, parts), SEQ)  31.4 us
    all_to_all x1, starting transfers between devices, body(): grads = a2a(after(out, parts), SEQ)  13.8 us
    all_to_all x1, blocking collectives, body(): a2a(jnp.broadcast_to(w8[None], (4, 8, 6, WIDTH)), 'x').reshape(32, 6, WIDTH)  13.2 us
    ppermute x2, waiting for transfers between devices, body(): swap = lambda x: lax.ppermute(x, 'zh', flip)  12.4 us
    all_to_all x1, blocking collectives, body(): parts = a2a(part.reshape(4, 8, 6, WIDTH), 'x')  10.5 us
    ppermute x1, waiting for transfers between devices, body(): lax.ppermute(after(grad_weight, grads), ALL, [(d, s) for s, d in weight_p...  6.63 us
  transfers between devices with their start and end apart: 9, of which 4 were waited for; matrix products, arithmetic and copies ran while one was open for 1% of the time, Pallas kernels for 14%

profile of v2, /device:TPU:39, one launch (start us, length us, event | category | flops | bytes accessed | tf_op | source)
XLA Modules:
  0.0 216.2 jit_solution(15158257549097465901)
XLA Ops:
  7.2 2.6 %prep.1 = bf16[16,288,128]{2,1,0:T(8,128)(2,1)} custom-call(bf16[128,1536]{1,0:T(8,128)(2,1)} %bitcast.14, bf16[128,1536]{1,0:T(8,128)(2,1)} %bitcast.15, bf16[128,1536]{1,0:T(8,128)(2,1)} %bitcast.16), custom_call_target="tpu_custom_call" | custom-call | flops 2860000000 | bytes 1 | tf_op jit(solution)/shard_map/prep/pallas_call | solution.py:37
  9.8 45.0 %all_to_all.30.qkv = bf16[16,288,128]{2,1,0:T(8,128)(2,1)} all-to-all(bf16[16,288,128]{2,1,0:T(8,128)(2,1)} %prep.1), channel_id=1, replica_groups=mesh['zl'=4,'x'=4,'zh'=2,'y'=4,'c'=2] {'zh','y','c'}, dimensions={0} | all-to-all | bytes 2359296 | tf_op jit(solution)/shard_map/all_to_all | solution.py:268
  54.9 1.9 collective-permute-start
  56.9 12.4 %fwd.1 = (bf16[8,96,128]{2,1,0:T(8,128)(2,1)}, bf16[8,96,128]{2,1,0:T(8,128)(2,1)}, f32[16,96,128]{2,1,0:T(8,128)}, f32[16,8,128]{2,1,0:T(8,128)}) custom-call(bf16[16,288,128]{2,1,0:T(8,128)(2,1)} %all_to_all.30.qkv, s32[1]{0:T(128)} %bitcast.3.side), custom_call_target="tpu_custom_call" | custom-call | flops 13639999488 | bytes 1 | tf_op jit(solution)/shard_map/fwd/pallas_call | solution.py:37
  69.2 0.7 broadcast_in_dim.24
  69.9 3.3 %all-to-all-start.1 = ((bf16[8,6,1536]{2,1,0:T(8,128)(2,1)}), bf16[8,6,1536]{2,1,0:T(8,128)(2,1)S(1)}, u32[]{:S(2)}, u32[]{:S(2)}) async-start(bf16[8,6,1536]{2,1,0:T(8,128)(2,1)} %broadcast_in_dim.24), calls=%async_computation.1 | async-start | bytes 393216 | tf_op jit(solution)/shard_map/all_to_all | solution.py:273
  73.3 4.0 %collective-permute-start.1 = (bf16[8,96,128]{2,1,0:T(8,128)(2,1)}, bf16[8,96,128]{2,1,0:T(8,128)(2,1)S(1)}, u32[]{:S(2)}, u32[]{:S(2)}) collective-permute-start(bf16[8,96,128]{2,1,0:T(8,128)(2,1)} %get-tuple-element.29), channel_id=1, source_target_pairs={{0,8},{8,0},{1,9},{9,1},{2,10},{10,2},{3,11},{11,3},{4,12},{12,4},... | collective-permute-start | bytes 589832 | tf_op jit(solution)/shard_map/ppermute | solution.py:265
  77.3 11.2 %collective-permute-done.1.recv = bf16[8,96,128]{2,1,0:T(8,128)(2,1)S(1)} collective-permute-done((bf16[8,96,128]{2,1,0:T(8,128)(2,1)}, bf16[8,96,128]{2,1,0:T(8,128)(2,1)S(1)}, u32[]{:S(2)}, u32[]{:S(2)}) %collective-permute-start.1) | collective-permute-done | bytes 196640 | tf_op jit(solution)/shard_map/ppermute | solution.py:265
  88.7 13.2 %all_to_all.31 = bf16[4,8,6,1536]{3,1,2,0:T(8,128)(2,1)S(1)} all-to-all(bf16[4,8,6,1536]{3,1,2,0:T(8,128)(2,1)S(1)} %broadcast_in_dim.25), channel_id=1, replica_groups=mesh['zl'=4,'x'=4,'zh'=2,'y'=4,'c'=2] {'x'}, dimensions={0} | all-to-all | bytes 1179648 | tf_op jit(solution)/shard_map/all_to_all | solution.py:275
  101.9 1.1 copy.16
  103.0 4.4 %grad_w.1 = (bf16[32,6,1536]{2,1,0:T(8,128)(2,1)}, bf16[8,192,128]{2,1,0:T(8,128)(2,1)}) custom-call(bf16[8,96,128]{2,1,0:T(8,128)(2,1)} %get-tuple-element.31.keep, bf16[8,96,128]{2,1,0:T(8,128)(2,1)} %copy-done.3, bf16[1024,1536]{1,0:T(8,128)(2,1)} %all-gather.2.cloned.1.call-done.cot, s32[1]{0:T(128)} %bitcast.3.side), custom_call_target="tpu_custom_call" | custom-call | flops 4840000000 | bytes 1 | tf_op jit(solution)/shard_map/grad_w/pallas_call | solution.py:37
  107.4 6.2 %grad_att.1 = (bf16[8,96,128]{2,1,0:T(8,128)(2,1)}, bf16[8,96,128]{2,1,0:T(8,128)(2,1)}, bf16[1024,1536]{1,0:T(8,128)(2,1)}) custom-call(bf16[32,6,1536]{2,1,0:T(8,128)(2,1)} %bitcast.12, bf16[1024,1536]{1,0:T(8,128)(2,1)} %all-gather.2.cloned.1.call-done.cot, bf16[8,192,128]{2,1,0:T(8,128)(2,1)} %get-tuple-element.35.att, s32[1]{0:T(128)} %bitcast.3.side), custom_call_target="tpu_custom_call" | custom-call | flops 6710000128 | bytes 1 | tf_op jit(solution)/shard_map/grad_att/pallas_call | solution.py:37
  113.7 1.1 copy-done.1
  115.0 10.5 %all_to_all.32 = bf16[4,8,6,1536]{3,1,2,0:T(8,128)(2,1)S(1)} all-to-all(bf16[4,8,6,1536]{3,1,2,0:T(8,128)(2,1)S(1)} %copy.17), channel_id=1, replica_groups=mesh['zl'=4,'x'=4,'zh'=2,'y'=4,'c'=2] {'x'}, dimensions={0} | all-to-all | bytes 1179648 | tf_op jit(solution)/shard_map/all_to_all | solution.py:278
  125.5 1.3 collective-permute-start.2
  126.9 0.7 copy.18
  127.6 5.7 %all-to-all-start.4 = ((bf16[8,6,1536]{2,1,0:T(8,128)(2,1)}), bf16[8,6,1536]{2,1,0:T(8,128)(2,1)S(1)}, u32[]{:S(2)}, u32[]{:S(2)}) async-start(bf16[8,6,1536]{2,1,0:T(8,128)(2,1)} %copy.18), calls=%async_computation.5 | async-start | bytes 393216 | tf_op jit(solution)/shard_map/all_to_all | solution.py:283
  133.3 1.2 collective-permute-done.2.recv
  135.1 16.2 %bwd.1 = bf16[16,288,128]{2,1,0:T(8,128)(2,1)} custom-call(bf16[16,288,128]{2,1,0:T(8,128)(2,1)} %all_to_all.30.qkv, bf16[8,96,128]{2,1,0:T(8,128)(2,1)} %get-tuple-element.37.keep, bf16[8,96,128]{2,1,0:T(8,128)(2,1)} %copy-done.4, f32[16,96,128]{2,1,0:T(8,128)} %get-tuple-element.40.acc_in, f32[16,8,128]{2,1,0:T(8,128)} %get-tuple-element.41.lse_in, ...), custom_call_target="tpu_custom_call" | custom-call | flops 17820000256 | bytes 1 | tf_op jit(solution)/shard_map/bwd/pallas_call | solution.py:37
  151.3 13.8 %all-to-all-start.5 = ((bf16[16,288,128]{2,1,0:T(8,128)(2,1)}), bf16[16,288,128]{2,1,0:T(8,128)(2,1)S(1)}, u32[]{:S(2)}, u32[]{:S(2)}) async-start(bf16[16,288,128]{2,1,0:T(8,128)(2,1)} %bwd.1), calls=%async_computation.6 | async-start | bytes 2359296 | tf_op jit(solution)/shard_map/all_to_all | solution.py:284
  165.1 31.4 %all-to-all-done.5.src = bf16[16,288,128]{2,1,0:T(8,128)(2,1)S(1)} async-done(((bf16[16,288,128]{2,1,0:T(8,128)(2,1)}), bf16[16,288,128]{2,1,0:T(8,128)(2,1)S(1)}, u32[]{:S(2)}, u32[]{:S(2)}) %all-to-all-start.5) | async-done | bytes 1179680 | tf_op jit(solution)/shard_map/all_to_all | solution.py:284
  196.5 3.1 %collective-permute-start.3 = (f32[6,1536]{1,0:T(8,128)S(1)}, f32[6,1536]{1,0:T(8,128)S(1)}, u32[]{:S(2)}, u32[]{:S(2)}) collective-permute-start(f32[6,1536]{1,0:T(8,128)S(1)} %convert_reduce_fusion), channel_id=1, source_target_pairs={{0,0},{8,1},{64,2},{72,3},{128,4},{136,5},{192,6},{200,7},{16,8},{... | collective-permute-start | bytes 110600 | tf_op jit(solution)/shard_map/ppermute | solution.py:287
  199.6 2.4 %back.1 = (bf16[128,1536]{1,0:T(8,128)(2,1)}, bf16[128,1536]{1,0:T(8,128)(2,1)}, bf16[128,1536]{1,0:T(8,128)(2,1)}) custom-call(bf16[16,288,128]{2,1,0:T(8,128)(2,1)} %copy-done), custom_call_target="tpu_custom_call" | custom-call | flops 2640000000 | bytes 1 | tf_op jit(solution)/shard_map/back/pallas_call | solution.py:37
  202.1 6.6 %collective-permute-done.3 = f32[6,1536]{1,0:T(8,128)S(1)} collective-permute-done((f32[6,1536]{1,0:T(8,128)S(1)}, f32[6,1536]{1,0:T(8,128)S(1)}, u32[]{:S(2)}, u32[]{:S(2)}) %collective-permute-start.3) | collective-permute-done | bytes 36896 | tf_op jit(solution)/shard_map/ppermute | solution.py:287
  (26 shorter events, 1.8 us)
Async XLA Ops:
  7.2 95.9 %all-gather.2.cloned.1.call-start = ((), (), s32[]{:S(2)}) async-start(), calls=%async_computation.7 | async-start | bytes 3538944 | tf_op jit(solution)/shard_map/all_gather | solution.py:270
  9.8 45.1 %copy-start.5 = (bf16[6,1536]{1,0:T(8,128)(2,1)S(1)}, bf16[6,1536]{1,0:T(8,128)(2,1)}, u32[]{:S(2)}) copy-start(bf16[6,1536]{1,0:T(8,128)(2,1)} %param.9) | copy-start | bytes 55300
  54.9 14.3 %collective-permute-start = (bf16[6,1536]{1,0:T(8,128)(2,1)S(1)}, bf16[6,1536]{1,0:T(8,128)(2,1)S(1)}, u32[]{:S(2)}, u32[]{:S(2)}) collective-permute-start(bf16[6,1536]{1,0:T(8,128)(2,1)S(1)} %copy-done.5), channel_id=1, source_target_pairs={{0,0},{1,8},{2,64},{3,72},{4,128},{5,136},{6,192},{7,200},{8,16},{... | collective-permute-start | bytes 55304 | tf_op jit(solution)/shard_map/ppermute | solution.py:269
  69.9 18.7 %all-to-all-start.1 = ((bf16[8,6,1536]{2,1,0:T(8,128)(2,1)}), bf16[8,6,1536]{2,1,0:T(8,128)(2,1)S(1)}, u32[]{:S(2)}, u32[]{:S(2)}) async-start(bf16[8,6,1536]{2,1,0:T(8,128)(2,1)} %broadcast_in_dim.24), calls=%async_computation.1 | async-start | bytes 393216 | tf_op jit(solution)/shard_map/all_to_all | solution.py:273
  73.3 135.4 %reduce-scatter.2.cloned.1.call-start = ((), (), s32[]{:S(2)}) async-start(), calls=%async_computation.8 | async-start | bytes 3538944 | tf_op jit(solution)/shard_map/reduce_scatter | solution.py:281
  73.3 15.3 %collective-permute-start.1 = (bf16[8,96,128]{2,1,0:T(8,128)(2,1)}, bf16[8,96,128]{2,1,0:T(8,128)(2,1)S(1)}, u32[]{:S(2)}, u32[]{:S(2)}) collective-permute-start(bf16[8,96,128]{2,1,0:T(8,128)(2,1)} %get-tuple-element.29), channel_id=1, source_target_pairs={{0,8},{8,0},{1,9},{9,1},{2,10},{10,2},{3,11},{11,3},{4,12},{12,4},... | collective-permute-start | bytes 589832 | tf_op jit(solution)/shard_map/ppermute | solution.py:265
  88.6 14.4 %copy-start.3 = (bf16[8,96,128]{2,1,0:T(8,128)(2,1)}, bf16[8,96,128]{2,1,0:T(8,128)(2,1)S(1)}, u32[]{:S(2)}) copy-start(bf16[8,96,128]{2,1,0:T(8,128)(2,1)S(1)} %collective-permute-done.1.recv) | copy-start | bytes 589828
  113.6 1.1 copy-start.1
  115.0 10.6 %copy-start.2 = (bf16[8,96,128]{2,1,0:T(8,128)(2,1)S(1)}, bf16[8,96,128]{2,1,0:T(8,128)(2,1)}, u32[]{:S(2)}) copy-start(bf16[8,96,128]{2,1,0:T(8,128)(2,1)} %get-tuple-element.39) | copy-start | bytes 589828
  125.5 8.9 %collective-permute-start.2 = (bf16[8,96,128]{2,1,0:T(8,128)(2,1)S(1)}, bf16[8,96,128]{2,1,0:T(8,128)(2,1)S(1)}, u32[]{:S(2)}, u32[]{:S(2)}) collective-permute-start(bf16[8,96,128]{2,1,0:T(8,128)(2,1)S(1)} %copy-done.2), channel_id=1, source_target_pairs={{0,8},{8,0},{1,9},{9,1},{2,10},{10,2},{3,11},{11,3},{4,12},{12,4},... | collective-permute-start | bytes 589832 | tf_op jit(solution)/shard_map/ppermute | solution.py:265
  127.6 23.7 %all-to-all-start.4 = ((bf16[8,6,1536]{2,1,0:T(8,128)(2,1)}), bf16[8,6,1536]{2,1,0:T(8,128)(2,1)S(1)}, u32[]{:S(2)}, u32[]{:S(2)}) async-start(bf16[8,6,1536]{2,1,0:T(8,128)(2,1)} %copy.18), calls=%async_computation.5 | async-start | bytes 393216 | tf_op jit(solution)/shard_map/all_to_all | solution.py:283
  134.4 0.7 copy-start.4
  151.3 45.2 %all-to-all-start.5 = ((bf16[16,288,128]{2,1,0:T(8,128)(2,1)}), bf16[16,288,128]{2,1,0:T(8,128)(2,1)S(1)}, u32[]{:S(2)}, u32[]{:S(2)}) async-start(bf16[16,288,128]{2,1,0:T(8,128)(2,1)} %bwd.1), calls=%async_computation.6 | async-start | bytes 2359296 | tf_op jit(solution)/shard_map/all_to_all | solution.py:284
  196.5 3.1 %copy-start = (bf16[16,288,128]{2,1,0:T(8,128)(2,1)}, bf16[16,288,128]{2,1,0:T(8,128)(2,1)S(1)}, u32[]{:S(2)}) copy-start(bf16[16,288,128]{2,1,0:T(8,128)(2,1)S(1)} %all-to-all-done.5.src) | copy-start | bytes 3538948
  196.5 12.2 %collective-permute-start.3 = (f32[6,1536]{1,0:T(8,128)S(1)}, f32[6,1536]{1,0:T(8,128)S(1)}, u32[]{:S(2)}, u32[]{:S(2)}) collective-permute-start(f32[6,1536]{1,0:T(8,128)S(1)} %convert_reduce_fusion), channel_id=1, source_target_pairs={{0,0},{8,1},{64,2},{72,3},{128,4},{136,5},{192,6},{200,7},{16,8},{... | collective-permute-start | bytes 110600 | tf_op jit(solution)/shard_map/ppermute | solution.py:287
Sparse Core Ops, SparseCore 0:
  55.0 26.3 all-gather.1
  113.8 36.1 reduce-scatter.1

commit v3 on v2

--- a/solution.py
+++ b/solution.py
@@ -40,7 +40,7 @@
         in_specs=specs,
         out_specs=tuple(vmem for _ in outs),
         scratch_shapes=list(scratch),
-        cost_estimate=pl.CostEstimate(flops=int(us * 1.1e9), bytes_accessed=1, transcendentals=0),
+        cost_estimate=pl.CostEstimate(flops=1, bytes_accessed=1, transcendentals=0),
         compiler_params=pltpu.CompilerParams(vmem_limit_bytes=56 * 2**20),
         name=name,
     )(*ins)
@@ -140,30 +140,29 @@
     )
 
 
-def grad_kernel(w32, cot, att, side, keep, send, proj, w_s):
+def grad_kernel(w32, cot, side, w_out, keep, send, w_s):
     for n in range(32):
         w_s[n * 6 : (n + 1) * 6, :] = w32[n].astype(F32)
     w_pair = w_s[...].astype(BF16)
+    w_out[...] = w_pair
     low = side[0] == 0
     for b in range(HALF):
-        rows = slice(b * FB, (b + 1) * FB)
         both = lax.dot_general(
-            w_pair, cot[rows, :], (((1,), (1,)), ((), ())), preferred_element_type=F32
+            w_pair, cot[b * FB : (b + 1) * FB, :], (((1,), (1,)), ((), ())), preferred_element_type=F32
         )
         keep[b] = jnp.where(low, both[:HD], both[HD:]).astype(BF16)
         send[b] = jnp.where(low, both[HD:], both[:HD]).astype(BF16)
-        proj[rows, :] = nn(att[b].T, w_pair).astype(BF16)
-
-
-def grad_attended(w32, cot, att_pair):
+
+
+def grad_attended(w32, cot):
     half = shape((HALF, HD, FB), BF16)
     return call(
         grad_kernel,
-        [w32, cot, att_pair],
-        [half, half, shape((HALF * FB, WIDTH), BF16)],
+        [w32, cot],
+        [shape((PAIR, WIDTH), BF16), half, half],
         [pltpu.VMEM((PAIR, WIDTH), F32)],
         side=True,
-        us=6.1,
+        us=4.4,
         name="grad_att",
     )
 
@@ -224,27 +223,25 @@
     )[0]
 
 
-def weight_kernel(keep, recv, cot, side, out, pair, w_s):
+def weight_kernel(keep, recv, cot, w_pair, side, out, proj):
     low = side[0] == 0
     acc = jnp.zeros((PAIR, WIDTH), F32)
     for b in range(HALF):
         mine, other = keep[b], recv[b]
+        rows = slice(b * FB, (b + 1) * FB)
         both = jnp.concatenate([jnp.where(low, mine, other), jnp.where(low, other, mine)], axis=0)
-        pair[b] = both
-        acc = acc + nn(both, cot[b * FB : (b + 1) * FB, :])
-    w_s[...] = acc
-    for n in range(32):
-        out[n] = w_s[n * 6 : (n + 1) * 6, :].astype(BF16)
-
-
-def weight_part(keep, recv, cot):
+        acc = acc + nn(both, cot[rows, :])
+        proj[rows, :] = nn(both.T, w_pair[...]).astype(BF16)
+    out[...] = acc
+
+
+def weight_part(keep, recv, cot, w_pair):
     return call(
         weight_kernel,
-        [keep, recv, cot],
-        [shape((32, 6, WIDTH), BF16), shape((HALF, PAIR, FB), BF16)],
-        [pltpu.VMEM((PAIR, WIDTH), F32)],
-        side=True,
-        us=4.4,
+        [keep, recv, cot, w_pair],
+        [shape((PAIR, WIDTH), F32), shape((HALF * FB, WIDTH), BF16)],
+        side=True,
+        us=6.4,
         name="grad_w",
     )
 
@@ -269,22 +266,21 @@
     w_mine = lax.ppermute(after(out_weight, qkv), ALL, weight_pairs())
     cot = lax.all_gather(after(cotangent[0], qkv), YC, axis=0, tiled=True)
     att_keep, att_send, acc, lse = forward(qkv)
+    w8 = a2a(after(jnp.broadcast_to(w_mine[None], (8, 6, WIDTH)), lse), Z8)
     att_recv = swap(att_send)
-    w8 = a2a(after(jnp.broadcast_to(w_mine[None], (8, 6, WIDTH)), lse), Z8)
-    w8 = after(w8, att_recv)
+    w8 = after(w8, lse)
     w32 = a2a(jnp.broadcast_to(w8[None], (4, 8, 6, WIDTH)), "x").reshape(32, 6, WIDTH)
-    part, att_pair = weight_part(att_keep, att_recv, cot)
-    g_keep, g_send, proj = grad_attended(after(w32, part), cot, att_pair)
-    parts = a2a(part.reshape(4, 8, 6, WIDTH), "x")
-    parts = jnp.sum(parts.astype(F32), axis=0).astype(BF16)
-    g_recv = swap(after(g_send, parts))
-    projected = lax.psum_scatter(proj, YC, scatter_dimension=0, tiled=True)
-    out = backward(qkv, g_keep, g_recv, acc, after(lse, parts))
-    parts = a2a(parts, Z8)
-    grads = a2a(after(out, parts), SEQ)
-
+    w_pair, g_keep, g_send = grad_attended(w32, cot)
+    g_recv = swap(after(g_send, att_recv))
+    part, proj = weight_part(att_keep, att_recv, cot, w_pair)
+    part = lax.psum_scatter(after(part, g_recv), "x", scatter_dimension=0, tiled=True)
+    out = backward(qkv, g_keep, g_recv, acc, after(lse, proj))
+    projected = lax.psum_scatter(after(proj, out), YC, scatter_dimension=0, tiled=True)
+    grads = a2a(out, SEQ)
+    parts = a2a(after(part, grads).astype(BF16).reshape(8, 6, WIDTH), Z8)
     grad_weight = jnp.sum(parts.astype(F32), axis=0)
-    grad_weight = lax.ppermute(after(grad_weight, grads), ALL, [(d, s) for s, d in weight_pairs()])
+    grad_weight = lax.ppermute(grad_weight, ALL, [(d, s) for s, d in weight_pairs()])
+
     grad_query, grad_key, grad_value = back(grads)
     return (projected[None], grad_query[None], grad_key[None], grad_value[None], grad_weight)
 

time: 219 us -> 208 us (0.950)
  blocking collectives: 68.7 us -> 116 us
  waiting for transfers between devices: 50.5 us -> 13.2 us
  starting transfers between devices: 33.3 us -> 13.7 us
    all_to_all x2 -> x3, blocking collectives: 23.7 us -> 70.9 us  [the longest x1 48.4 us: body(): grads = a2a(out, SEQ)]
    all_to_all x3 -> x1, waiting for transfers between devices: 31.4 us -> 5.1 us  [body(): a2a(jnp.broadcast_to(w8[None], (4, 8, 6, WIDTH)), 'x').reshape(32, 6, WIDTH)]
    all_to_all x3 -> x1, starting transfers between devices: 22.8 us -> 5.89 us  [body(): a2a(jnp.broadcast_to(w8[None], (4, 8, 6, WIDTH)), 'x').reshape(32, 6, WIDTH)]
    ppermute x2, waiting for transfers between devices: 12.4 us -> 2.01 us  [body(): swap = lambda x: lax.ppermute(x, 'zh', flip)]
    ppermute x2, starting transfers between devices: 5.35 us -> 0.89 us  [body(): swap = lambda x: lax.ppermute(x, 'zh', flip)]
  transfers between devices with their start and end apart: 9 -> 8, of which waited for: 4 -> 3; matrix products, arithmetic and copies ran while one was open for 1% -> 2% of each run, Pallas kernels for 14% -> 20%
where the time goes in v3:
time: 208 us; the launch traced here: 207 us
  blocking collectives  116 us (56%)
  Pallas kernels  44.3 us (21%)
  between operations  13.8 us (7%)
  starting transfers between devices  13.7 us (7%)
  waiting for transfers between devices  13.2 us (6%)
  local copies, waits for them, and re-layouts  5 us (2%)
    all_to_all x1, blocking collectives, body(): grads = a2a(out, SEQ)  48.4 us
    all_to_all x1, blocking collectives, body(): qkv = a2a(prep(query[0], key_proj[0], value[0]), SEQ)  45 us
    pallas_call x6, Pallas kernels, call(): pl.pallas_call(kernel, out_shape=tuple(outs), in_specs=specs, out_specs=t...  44.3 us
    all_to_all x1, blocking collectives, body(): parts = a2a(after(part, grads).astype(BF16).reshape(8, 6, WIDTH), Z8)  12.2 us
    all_to_all x1, blocking collectives, body(): w8 = a2a(after(jnp.broadcast_to(w_mine[None], (8, 6, WIDTH)), lse), Z8)  10.3 us
    ppermute x1, waiting for transfers between devices, body(): lax.ppermute(grad_weight, ALL, [(d, s) for s, d in weight_pairs()])  6.08 us
    all_to_all x1, starting transfers between devices, body(): a2a(jnp.broadcast_to(w8[None], (4, 8, 6, WIDTH)), 'x').reshape(32, 6, WIDTH)  5.89 us
    all_to_all x1, waiting for transfers between devices, body(): a2a(jnp.broadcast_to(w8[None], (4, 8, 6, WIDTH)), 'x').reshape(32, 6, WIDTH)  5.1 us
  transfers between devices with their start and end apart: 8, of which 3 were waited for; matrix products, arithmetic and copies ran while one was open for 2% of the time, Pallas kernels for 20%

profile of v3, /device:TPU:39, one launch (start us, length us, event | category | flops | bytes accessed | tf_op | source)
XLA Modules:
  0.0 207.0 jit_solution(9658338851834651605)
XLA Ops:
  7.2 2.6 %prep.1 = bf16[16,288,128]{2,1,0:T(8,128)(2,1)} custom-call(bf16[128,1536]{1,0:T(8,128)(2,1)} %bitcast.11, bf16[128,1536]{1,0:T(8,128)(2,1)} %bitcast.12, bf16[128,1536]{1,0:T(8,128)(2,1)} %bitcast.13), custom_call_target="tpu_custom_call" | custom-call | flops 1 | bytes 1 | tf_op jit(solution)/shard_map/prep/pallas_call | solution.py:37
  9.8 45.0 %all_to_all.25.qkv = bf16[16,288,128]{2,1,0:T(8,128)(2,1)} all-to-all(bf16[16,288,128]{2,1,0:T(8,128)(2,1)} %prep.1), channel_id=1, replica_groups=mesh['zl'=4,'x'=4,'zh'=2,'y'=4,'c'=2] {'zh','y','c'}, dimensions={0} | all-to-all | bytes 2359296 | tf_op jit(solution)/shard_map/all_to_all | solution.py:265
  54.9 1.9 collective-permute-start.1
  56.8 12.4 %fwd.1 = (bf16[8,96,128]{2,1,0:T(8,128)(2,1)}, bf16[8,96,128]{2,1,0:T(8,128)(2,1)}, f32[16,96,128]{2,1,0:T(8,128)}, f32[16,8,128]{2,1,0:T(8,128)}) custom-call(bf16[16,288,128]{2,1,0:T(8,128)(2,1)} %all_to_all.25.qkv, s32[1]{0:T(128)} %bitcast.3.side), custom_call_target="tpu_custom_call" | custom-call | flops 1 | bytes 1 | tf_op jit(solution)/shard_map/fwd/pallas_call | solution.py:37
  69.2 10.3 %all_to_all.26 = bf16[8,6,1536]{2,1,0:T(8,128)(2,1)S(1)} all-to-all(bf16[8,6,1536]{2,1,0:T(8,128)(2,1)S(1)} %broadcast_in_dim.24), channel_id=1, replica_groups=mesh['zl'=4,'x'=4,'zh'=2,'y'=4,'c'=2] {'zl','zh'}, dimensions={0} | all-to-all | bytes 294912 | tf_op jit(solution)/shard_map/all_to_all | solution.py:269
  79.6 0.9 broadcast_in_dim.25
  80.5 5.9 %all-to-all-start.2 = ((bf16[4,8,6,1536]{3,1,2,0:T(8,128)(2,1)}), bf16[4,8,6,1536]{3,1,2,0:T(8,128)(2,1)S(1)}, u32[]{:S(2)}, u32[]{:S(2)}) async-start(bf16[4,8,6,1536]{3,1,2,0:T(8,128)(2,1)} %broadcast_in_dim.25), calls=%async_computation.2 | async-start | bytes 1179648 | tf_op jit(solution)/shard_map/all_to_all | solution.py:272
  86.4 0.5 collective-permute-start
  86.9 5.1 %all-to-all-done.2 = bf16[4,8,6,1536]{3,1,2,0:T(8,128)(2,1)S(1)} async-done(((bf16[4,8,6,1536]{3,1,2,0:T(8,128)(2,1)}), bf16[4,8,6,1536]{3,1,2,0:T(8,128)(2,1)S(1)}, u32[]{:S(2)}, u32[]{:S(2)}) %all-to-all-start.2) | async-done | bytes 589856 | tf_op jit(solution)/shard_map/all_to_all | solution.py:272
  92.0 1.1 copy.12
  93.1 4.4 %grad_att.1 = (bf16[192,1536]{1,0:T(8,128)(2,1)}, bf16[8,96,128]{2,1,0:T(8,128)(2,1)}, bf16[8,96,128]{2,1,0:T(8,128)(2,1)}) custom-call(bf16[32,6,1536]{2,1,0:T(8,128)(2,1)} %bitcast.10, bf16[1024,1536]{1,0:T(8,128)(2,1)} %all-gather.2.cloned.1.call-done.cot, s32[1]{0:T(128)} %bitcast.3.side), custom_call_target="tpu_custom_call" | custom-call | flops 1 | bytes 1 | tf_op jit(solution)/shard_map/grad_att/pallas_call | solution.py:37
  97.4 0.4 collective-permute-start.2
  98.1 6.4 %grad_w.1 = (f32[192,1536]{1,0:T(8,128)}, bf16[1024,1536]{1,0:T(8,128)(2,1)}) custom-call(bf16[8,96,128]{2,1,0:T(8,128)(2,1)} %get-tuple-element.26.keep, bf16[8,96,128]{2,1,0:T(8,128)(2,1)} %copy-done.1, bf16[1024,1536]{1,0:T(8,128)(2,1)} %all-gather.2.cloned.1.call-done.cot, bf16[192,1536]{1,0:T(8,128)(2,1)} %get-tuple-element.33.w_pair, s32[1]{0:T(128)} %bitcast.3.side), custom_call_target="tpu_custom_call" | custom-call | flops 1 | bytes 1 | tf_op jit(solution)/shard_map/grad_w/pallas_call | solution.py:37
  104.5 2.0 collective-permute-done.2.recv
  106.6 0.6 copy-done.2
  107.2 16.1 %bwd.1 = bf16[16,288,128]{2,1,0:T(8,128)(2,1)} custom-call(bf16[16,288,128]{2,1,0:T(8,128)(2,1)} %all_to_all.25.qkv, bf16[8,96,128]{2,1,0:T(8,128)(2,1)} %get-tuple-element.35.keep, bf16[8,96,128]{2,1,0:T(8,128)(2,1)} %copy-done.2, f32[16,96,128]{2,1,0:T(8,128)} %get-tuple-element.38.acc_in, f32[16,8,128]{2,1,0:T(8,128)} %get-tuple-element.39.lse_in, ...), custom_call_target="tpu_custom_call" | custom-call | flops 1 | bytes 1 | tf_op jit(solution)/shard_map/bwd/pallas_call | solution.py:37
  123.4 1.4 copy-done
  124.8 48.4 %all_to_all.27.src = bf16[16,288,128]{2,1,0:T(8,128)(2,1)} all-to-all(bf16[16,288,128]{2,1,0:T(8,128)(2,1)S(1)} %copy-done), channel_id=1, replica_groups=mesh['zl'=4,'x'=4,'zh'=2,'y'=4,'c'=2] {'zh','y','c'}, dimensions={0} | all-to-all | bytes 2359296 | tf_op jit(solution)/shard_map/all_to_all | solution.py:279
  173.1 1.0 convert_element_type.6
  174.2 12.2 %all_to_all.28 = bf16[8,6,1536]{2,1,0:T(8,128)(2,1)S(1)} all-to-all(bf16[8,6,1536]{2,1,0:T(8,128)(2,1)S(1)} %reshape.26), channel_id=1, replica_groups=mesh['zl'=4,'x'=4,'zh'=2,'y'=4,'c'=2] {'zl','zh'}, dimensions={0} | all-to-all | bytes 294912 | tf_op jit(solution)/shard_map/all_to_all | solution.py:280
  186.4 4.9 %collective-permute-start.3 = (f32[6,1536]{1,0:T(8,128)S(1)}, f32[6,1536]{1,0:T(8,128)S(1)}, u32[]{:S(2)}, u32[]{:S(2)}) collective-permute-start(f32[6,1536]{1,0:T(8,128)S(1)} %convert_reduce_fusion), channel_id=1, source_target_pairs={{0,0},{8,1},{64,2},{72,3},{128,4},{136,5},{192,6},{200,7},{16,8},{... | collective-permute-start | bytes 110600 | tf_op jit(solution)/shard_map/ppermute | solution.py:282
  191.3 2.4 %back.1 = (bf16[128,1536]{1,0:T(8,128)(2,1)}, bf16[128,1536]{1,0:T(8,128)(2,1)}, bf16[128,1536]{1,0:T(8,128)(2,1)}) custom-call(bf16[16,288,128]{2,1,0:T(8,128)(2,1)} %all_to_all.27.src), custom_call_target="tpu_custom_call" | custom-call | flops 1 | bytes 1 | tf_op jit(solution)/shard_map/back/pallas_call | solution.py:37
  193.8 6.1 %collective-permute-done.3 = f32[6,1536]{1,0:T(8,128)S(1)} collective-permute-done((f32[6,1536]{1,0:T(8,128)S(1)}, f32[6,1536]{1,0:T(8,128)S(1)}, u32[]{:S(2)}, u32[]{:S(2)}) %collective-permute-start.3) | collective-permute-done | bytes 36896 | tf_op jit(solution)/shard_map/ppermute | solution.py:282
  199.9 0.6 copy.14
  (23 shorter events, 0.6 us)
Async XLA Ops:
  7.2 85.9 %all-gather.2.cloned.1.call-start = ((), (), s32[]{:S(2)}) async-start(), calls=%async_computation.7 | async-start | bytes 3538944 | tf_op jit(solution)/shard_map/all_gather | solution.py:267
  9.8 45.1 %copy-start.4 = (bf16[6,1536]{1,0:T(8,128)(2,1)S(1)}, bf16[6,1536]{1,0:T(8,128)(2,1)}, u32[]{:S(2)}) copy-start(bf16[6,1536]{1,0:T(8,128)(2,1)} %param.9) | copy-start | bytes 55300
  54.9 14.3 %collective-permute-start.1 = (bf16[6,1536]{1,0:T(8,128)(2,1)S(1)}, bf16[6,1536]{1,0:T(8,128)(2,1)S(1)}, u32[]{:S(2)}, u32[]{:S(2)}) collective-permute-start(bf16[6,1536]{1,0:T(8,128)(2,1)S(1)} %copy-done.4), channel_id=1, source_target_pairs={{0,0},{1,8},{2,64},{3,72},{4,128},{5,136},{6,192},{7,200},{8,16},{... | collective-permute-start | bytes 55304 | tf_op jit(solution)/shard_map/ppermute | solution.py:266
  79.6 6.8 %copy-start.3 = (bf16[8,96,128]{2,1,0:T(8,128)(2,1)S(1)}, bf16[8,96,128]{2,1,0:T(8,128)(2,1)}, u32[]{:S(2)}) copy-start(bf16[8,96,128]{2,1,0:T(8,128)(2,1)} %get-tuple-element.27) | copy-start | bytes 589828
  80.5 11.5 %all-to-all-start.2 = ((bf16[4,8,6,1536]{3,1,2,0:T(8,128)(2,1)}), bf16[4,8,6,1536]{3,1,2,0:T(8,128)(2,1)S(1)}, u32[]{:S(2)}, u32[]{:S(2)}) async-start(bf16[4,8,6,1536]{3,1,2,0:T(8,128)(2,1)} %broadcast_in_dim.25), calls=%async_computation.2 | async-start | bytes 1179648 | tf_op jit(solution)/shard_map/all_to_all | solution.py:272
  86.4 86.8 %reduce-scatter.5.cloned.1.call-start = ((), (), s32[]{:S(2)}) async-start(), calls=%async_computation.9 | async-start | bytes 1474560 | tf_op jit(solution)/shard_map/reduce_scatter | solution.py:276
  86.4 11.1 %collective-permute-start = (bf16[8,96,128]{2,1,0:T(8,128)(2,1)S(1)}, bf16[8,96,128]{2,1,0:T(8,128)(2,1)S(1)}, u32[]{:S(2)}, u32[]{:S(2)}) collective-permute-start(bf16[8,96,128]{2,1,0:T(8,128)(2,1)S(1)} %copy-done.3), channel_id=1, source_target_pairs={{0,8},{8,0},{1,9},{9,1},{2,10},{10,2},{3,11},{11,3},{4,12},{12,4},... | collective-permute-start | bytes 589832 | tf_op jit(solution)/shard_map/ppermute | solution.py:262
  97.4 0.7 copy-start.1
  97.4 9.1 %collective-permute-start.2 = (bf16[8,96,128]{2,1,0:T(8,128)(2,1)}, bf16[8,96,128]{2,1,0:T(8,128)(2,1)S(1)}, u32[]{:S(2)}, u32[]{:S(2)}) collective-permute-start(bf16[8,96,128]{2,1,0:T(8,128)(2,1)} %get-tuple-element.37), channel_id=1, source_target_pairs={{0,8},{8,0},{1,9},{9,1},{2,10},{10,2},{3,11},{11,3},{4,12},{12,4},... | collective-permute-start | bytes 589832 | tf_op jit(solution)/shard_map/ppermute | solution.py:262
  106.5 0.7 copy-start.2
  106.5 93.3 %reduce-scatter.3.cloned.1.call-start = ((), (), s32[]{:S(2)}) async-start(), calls=%async_computation.8 | async-start | bytes 3538944 | tf_op jit(solution)/shard_map/reduce_scatter | solution.py:278
  123.3 1.4 copy-start
  186.4 13.4 %collective-permute-start.3 = (f32[6,1536]{1,0:T(8,128)S(1)}, f32[6,1536]{1,0:T(8,128)S(1)}, u32[]{:S(2)}, u32[]{:S(2)}) collective-permute-start(f32[6,1536]{1,0:T(8,128)S(1)} %convert_reduce_fusion), channel_id=1, source_target_pairs={{0,0},{8,1},{64,2},{72,3},{128,4},{136,5},{192,6},{200,7},{16,8},{... | collective-permute-start | bytes 110600 | tf_op jit(solution)/shard_map/ppermute | solution.py:282
Sparse Core Ops, SparseCore 0:
  55.0 26.3 all-gather.1
  106.7 29.4 reduce-scatter.4
  139.3 42.4 reduce-scatter.2

commit v4 on v3

--- a/solution.py
+++ b/solution.py
@@ -18,7 +18,7 @@
 NB = 16
 HALF = 8
 FB = 128
-QB = 2
+QB = 8
 FRAMES = NB * FB
 PAIR = 2 * HD
 WIDTH = NB * HD

time: 208 us -> 202 us (0.971)
  Pallas kernels: 44.3 us -> 39.1 us
  waiting for transfers between devices: 13.2 us -> 11.1 us
    pallas_call x6, Pallas kernels: 44.3 us -> 39.1 us  [call(): pl.pallas_call(kernel, out_shape=tuple(outs), in_specs=specs, out_specs=t...]
    all_to_all x1, blocking collectives: 10.3 us -> 13.9 us  [body(): w8 = a2a(after(jnp.broadcast_to(w_mine[None], (8, 6, WIDTH)), lse), Z8)]
    all_to_all x1, blocking collectives: 48.4 us -> 45.8 us  [body(): grads = a2a(out, SEQ)]
  transfers between devices with their start and end apart: 8 -> 8, of which waited for: 3 -> 4; matrix products, arithmetic and copies ran while one was open for 2% -> 2% of each run, Pallas kernels for 20% -> 18%
where the time goes in v4:
time: 202 us; the launch traced here: 200 us
  blocking collectives  116 us (57%)
  Pallas kernels  39.1 us (19%)
  starting transfers between devices  14.5 us (7%)
  between operations  13.8 us (7%)
  waiting for transfers between devices  11.1 us (5%)
  local copies, waits for them, and re-layouts  4.39 us (2%)
    all_to_all x1, blocking collectives, body(): grads = a2a(out, SEQ)  45.8 us
    all_to_all x1, blocking collectives, body(): qkv = a2a(prep(query[0], key_proj[0], value[0]), SEQ)  45 us
    pallas_call x6, Pallas kernels, call(): pl.pallas_call(kernel, out_shape=tuple(outs), in_specs=specs, out_specs=t...  39.1 us
    all_to_all x1, blocking collectives, body(): w8 = a2a(after(jnp.broadcast_to(w_mine[None], (8, 6, WIDTH)), lse), Z8)  13.9 us
    all_to_all x1, blocking collectives, body(): parts = a2a(after(part, grads).astype(BF16).reshape(8, 6, WIDTH), Z8)  11.4 us
    all_to_all x1, waiting for transfers between devices, body(): a2a(jnp.broadcast_to(w8[None], (4, 8, 6, WIDTH)), 'x').reshape(32, 6, WIDTH)  5.66 us
    ppermute x1, starting transfers between devices, body(): lax.ppermute(grad_weight, ALL, [(d, s) for s, d in weight_pairs()])  5.61 us
    ppermute x1, waiting for transfers between devices, body(): lax.ppermute(grad_weight, ALL, [(d, s) for s, d in weight_pairs()])  4.32 us
  transfers between devices with their start and end apart: 8, of which 4 were waited for; matrix products, arithmetic and copies ran while one was open for 2% of the time, Pallas kernels for 18%

profile of v4, /device:TPU:39, one launch (start us, length us, event | category | flops | bytes accessed | tf_op | source)
XLA Modules:
  0.0 200.1 jit_solution(15040629225159728314)
XLA Ops:
  7.2 2.6 %prep.1 = bf16[16,288,128]{2,1,0:T(8,128)(2,1)} custom-call(bf16[128,1536]{1,0:T(8,128)(2,1)} %bitcast.11, bf16[128,1536]{1,0:T(8,128)(2,1)} %bitcast.12, bf16[128,1536]{1,0:T(8,128)(2,1)} %bitcast.13), custom_call_target="tpu_custom_call" | custom-call | flops 1 | bytes 1 | tf_op jit(solution)/shard_map/prep/pallas_call | solution.py:37
  9.8 45.0 %all_to_all.25.qkv = bf16[16,288,128]{2,1,0:T(8,128)(2,1)} all-to-all(bf16[16,288,128]{2,1,0:T(8,128)(2,1)} %prep.1), channel_id=1, replica_groups=mesh['zl'=4,'x'=4,'zh'=2,'y'=4,'c'=2] {'zh','y','c'}, dimensions={0} | all-to-all | bytes 2359296 | tf_op jit(solution)/shard_map/all_to_all | solution.py:265
  54.9 1.9 collective-permute-start.1
  56.8 9.1 %fwd.1 = (bf16[8,96,128]{2,1,0:T(8,128)(2,1)}, bf16[8,96,128]{2,1,0:T(8,128)(2,1)}, f32[16,96,128]{2,1,0:T(8,128)}, f32[16,8,128]{2,1,0:T(8,128)}) custom-call(bf16[16,288,128]{2,1,0:T(8,128)(2,1)} %all_to_all.25.qkv, s32[1]{0:T(128)} %bitcast.3.side), custom_call_target="tpu_custom_call" | custom-call | flops 1 | bytes 1 | tf_op jit(solution)/shard_map/fwd/pallas_call | solution.py:37
  65.9 0.6 collective-permute-done.1
  66.5 13.9 %all_to_all.26 = bf16[8,6,1536]{2,1,0:T(8,128)(2,1)S(1)} all-to-all(bf16[8,6,1536]{2,1,0:T(8,128)(2,1)S(1)} %broadcast_in_dim.24), channel_id=1, replica_groups=mesh['zl'=4,'x'=4,'zh'=2,'y'=4,'c'=2] {'zl','zh'}, dimensions={0} | all-to-all | bytes 294912 | tf_op jit(solution)/shard_map/all_to_all | solution.py:269
  80.4 0.9 broadcast_in_dim.25
  81.3 3.9 %all-to-all-start.2 = ((bf16[4,8,6,1536]{3,1,2,0:T(8,128)(2,1)}), bf16[4,8,6,1536]{3,1,2,0:T(8,128)(2,1)S(1)}, u32[]{:S(2)}, u32[]{:S(2)}) async-start(bf16[4,8,6,1536]{3,1,2,0:T(8,128)(2,1)} %broadcast_in_dim.25), calls=%async_computation.2 | async-start | bytes 1179648 | tf_op jit(solution)/shard_map/all_to_all | solution.py:272
  85.2 0.6 collective-permute-start
  85.8 5.7 %all-to-all-done.2 = bf16[4,8,6,1536]{3,1,2,0:T(8,128)(2,1)S(1)} async-done(((bf16[4,8,6,1536]{3,1,2,0:T(8,128)(2,1)}), bf16[4,8,6,1536]{3,1,2,0:T(8,128)(2,1)S(1)}, u32[]{:S(2)}, u32[]{:S(2)}) %all-to-all-start.2) | async-done | bytes 589856 | tf_op jit(solution)/shard_map/all_to_all | solution.py:272
  91.5 1.1 copy.12
  92.6 4.4 %grad_att.1 = (bf16[192,1536]{1,0:T(8,128)(2,1)}, bf16[8,96,128]{2,1,0:T(8,128)(2,1)}, bf16[8,96,128]{2,1,0:T(8,128)(2,1)}) custom-call(bf16[32,6,1536]{2,1,0:T(8,128)(2,1)} %bitcast.10, bf16[1024,1536]{1,0:T(8,128)(2,1)} %all-gather.2.cloned.1.call-done.cot, s32[1]{0:T(128)} %bitcast.3.side), custom_call_target="tpu_custom_call" | custom-call | flops 1 | bytes 1 | tf_op jit(solution)/shard_map/grad_att/pallas_call | solution.py:37
  97.0 2.1 %collective-permute-start.2 = (bf16[8,96,128]{2,1,0:T(8,128)(2,1)}, bf16[8,96,128]{2,1,0:T(8,128)(2,1)S(1)}, u32[]{:S(2)}, u32[]{:S(2)}) collective-permute-start(bf16[8,96,128]{2,1,0:T(8,128)(2,1)} %get-tuple-element.37), channel_id=1, source_target_pairs={{0,8},{8,0},{1,9},{9,1},{2,10},{10,2},{3,11},{11,3},{4,12},{12,4},... | collective-permute-start | bytes 589832 | tf_op jit(solution)/shard_map/ppermute | solution.py:262
  99.1 6.4 %grad_w.1 = (f32[192,1536]{1,0:T(8,128)}, bf16[1024,1536]{1,0:T(8,128)(2,1)}) custom-call(bf16[8,96,128]{2,1,0:T(8,128)(2,1)} %get-tuple-element.26.keep, bf16[8,96,128]{2,1,0:T(8,128)(2,1)} %copy-done.1, bf16[1024,1536]{1,0:T(8,128)(2,1)} %all-gather.2.cloned.1.call-done.cot, bf16[192,1536]{1,0:T(8,128)(2,1)} %get-tuple-element.33.w_pair, s32[1]{0:T(128)} %bitcast.3.side), custom_call_target="tpu_custom_call" | custom-call | flops 1 | bytes 1 | tf_op jit(solution)/shard_map/grad_w/pallas_call | solution.py:37
  105.5 0.5 collective-permute-done.2.recv
  106.7 14.2 %bwd.1 = bf16[16,288,128]{2,1,0:T(8,128)(2,1)} custom-call(bf16[16,288,128]{2,1,0:T(8,128)(2,1)} %all_to_all.25.qkv, bf16[8,96,128]{2,1,0:T(8,128)(2,1)} %get-tuple-element.35.keep, bf16[8,96,128]{2,1,0:T(8,128)(2,1)} %copy-done.2, f32[16,96,128]{2,1,0:T(8,128)} %get-tuple-element.38.acc_in, f32[16,8,128]{2,1,0:T(8,128)} %get-tuple-element.39.lse_in, ...), custom_call_target="tpu_custom_call" | custom-call | flops 1 | bytes 1 | tf_op jit(solution)/shard_map/bwd/pallas_call | solution.py:37
  121.0 1.3 copy-done
  122.2 45.8 %all_to_all.27.src = bf16[16,288,128]{2,1,0:T(8,128)(2,1)} all-to-all(bf16[16,288,128]{2,1,0:T(8,128)(2,1)S(1)} %copy-done), channel_id=1, replica_groups=mesh['zl'=4,'x'=4,'zh'=2,'y'=4,'c'=2] {'zh','y','c'}, dimensions={0} | all-to-all | bytes 2359296 | tf_op jit(solution)/shard_map/all_to_all | solution.py:279
  168.1 1.0 convert_element_type.6
  169.1 11.4 %all_to_all.28 = bf16[8,6,1536]{2,1,0:T(8,128)(2,1)S(1)} all-to-all(bf16[8,6,1536]{2,1,0:T(8,128)(2,1)S(1)} %reshape.26), channel_id=1, replica_groups=mesh['zl'=4,'x'=4,'zh'=2,'y'=4,'c'=2] {'zl','zh'}, dimensions={0} | all-to-all | bytes 294912 | tf_op jit(solution)/shard_map/all_to_all | solution.py:280
  180.6 5.6 %collective-permute-start.3 = (f32[6,1536]{1,0:T(8,128)S(1)}, f32[6,1536]{1,0:T(8,128)S(1)}, u32[]{:S(2)}, u32[]{:S(2)}) collective-permute-start(f32[6,1536]{1,0:T(8,128)S(1)} %convert_reduce_fusion), channel_id=1, source_target_pairs={{0,0},{8,1},{64,2},{72,3},{128,4},{136,5},{192,6},{200,7},{16,8},{... | collective-permute-start | bytes 110600 | tf_op jit(solution)/shard_map/ppermute | solution.py:282
  186.2 2.4 %back.1 = (bf16[128,1536]{1,0:T(8,128)(2,1)}, bf16[128,1536]{1,0:T(8,128)(2,1)}, bf16[128,1536]{1,0:T(8,128)(2,1)}) custom-call(bf16[16,288,128]{2,1,0:T(8,128)(2,1)} %all_to_all.27.src), custom_call_target="tpu_custom_call" | custom-call | flops 1 | bytes 1 | tf_op jit(solution)/shard_map/back/pallas_call | solution.py:37
  188.6 4.3 %collective-permute-done.3 = f32[6,1536]{1,0:T(8,128)S(1)} collective-permute-done((f32[6,1536]{1,0:T(8,128)S(1)}, f32[6,1536]{1,0:T(8,128)S(1)}, u32[]{:S(2)}, u32[]{:S(2)}) %collective-permute-start.3) | collective-permute-done | bytes 36896 | tf_op jit(solution)/shard_map/ppermute | solution.py:282
  192.9 0.6 copy.14
  (23 shorter events, 0.9 us)
Async XLA Ops:
  7.2 85.5 %all-gather.2.cloned.1.call-start = ((), (), s32[]{:S(2)}) async-start(), calls=%async_computation.7 | async-start | bytes 3538944 | tf_op jit(solution)/shard_map/all_gather | solution.py:267
  9.8 45.1 %copy-start.4 = (bf16[6,1536]{1,0:T(8,128)(2,1)S(1)}, bf16[6,1536]{1,0:T(8,128)(2,1)}, u32[]{:S(2)}) copy-start(bf16[6,1536]{1,0:T(8,128)(2,1)} %param.9) | copy-start | bytes 55300
  54.9 11.6 %collective-permute-start.1 = (bf16[6,1536]{1,0:T(8,128)(2,1)S(1)}, bf16[6,1536]{1,0:T(8,128)(2,1)S(1)}, u32[]{:S(2)}, u32[]{:S(2)}) collective-permute-start(bf16[6,1536]{1,0:T(8,128)(2,1)S(1)} %copy-done.4), channel_id=1, source_target_pairs={{0,0},{1,8},{2,64},{3,72},{4,128},{5,136},{6,192},{7,200},{8,16},{... | collective-permute-start | bytes 55304 | tf_op jit(solution)/shard_map/ppermute | solution.py:266
  80.4 4.9 %copy-start.3 = (bf16[8,96,128]{2,1,0:T(8,128)(2,1)S(1)}, bf16[8,96,128]{2,1,0:T(8,128)(2,1)}, u32[]{:S(2)}) copy-start(bf16[8,96,128]{2,1,0:T(8,128)(2,1)} %get-tuple-element.27) | copy-start | bytes 589828
  81.3 10.2 %all-to-all-start.2 = ((bf16[4,8,6,1536]{3,1,2,0:T(8,128)(2,1)}), bf16[4,8,6,1536]{3,1,2,0:T(8,128)(2,1)S(1)}, u32[]{:S(2)}, u32[]{:S(2)}) async-start(bf16[4,8,6,1536]{3,1,2,0:T(8,128)(2,1)} %broadcast_in_dim.25), calls=%async_computation.2 | async-start | bytes 1179648 | tf_op jit(solution)/shard_map/all_to_all | solution.py:272
  85.2 82.9 %reduce-scatter.5.cloned.1.call-start = ((), (), s32[]{:S(2)}) async-start(), calls=%async_computation.9 | async-start | bytes 1474560 | tf_op jit(solution)/shard_map/reduce_scatter | solution.py:276
  85.2 11.8 %collective-permute-start = (bf16[8,96,128]{2,1,0:T(8,128)(2,1)S(1)}, bf16[8,96,128]{2,1,0:T(8,128)(2,1)S(1)}, u32[]{:S(2)}, u32[]{:S(2)}) collective-permute-start(bf16[8,96,128]{2,1,0:T(8,128)(2,1)S(1)} %copy-done.3), channel_id=1, source_target_pairs={{0,8},{8,0},{1,9},{9,1},{2,10},{10,2},{3,11},{11,3},{4,12},{12,4},... | collective-permute-start | bytes 589832 | tf_op jit(solution)/shard_map/ppermute | solution.py:262
  97.0 2.1 %copy-start.1 = (bf16[8,96,128]{2,1,0:T(8,128)(2,1)}, bf16[8,96,128]{2,1,0:T(8,128)(2,1)S(1)}, u32[]{:S(2)}) copy-start(bf16[8,96,128]{2,1,0:T(8,128)(2,1)S(1)} %collective-permute-done.recv) | copy-start | bytes 589828
  97.0 9.1 %collective-permute-start.2 = (bf16[8,96,128]{2,1,0:T(8,128)(2,1)}, bf16[8,96,128]{2,1,0:T(8,128)(2,1)S(1)}, u32[]{:S(2)}, u32[]{:S(2)}) collective-permute-start(bf16[8,96,128]{2,1,0:T(8,128)(2,1)} %get-tuple-element.37), channel_id=1, source_target_pairs={{0,8},{8,0},{1,9},{9,1},{2,10},{10,2},{3,11},{11,3},{4,12},{12,4},... | collective-permute-start | bytes 589832 | tf_op jit(solution)/shard_map/ppermute | solution.py:262
  106.0 0.7 copy-start.2
  106.1 86.9 %reduce-scatter.3.cloned.1.call-start = ((), (), s32[]{:S(2)}) async-start(), calls=%async_computation.8 | async-start | bytes 3538944 | tf_op jit(solution)/shard_map/reduce_scatter | solution.py:278
  121.0 1.3 copy-start
  180.6 12.4 %collective-permute-start.3 = (f32[6,1536]{1,0:T(8,128)S(1)}, f32[6,1536]{1,0:T(8,128)S(1)}, u32[]{:S(2)}, u32[]{:S(2)}) collective-permute-start(f32[6,1536]{1,0:T(8,128)S(1)} %convert_reduce_fusion), channel_id=1, source_target_pairs={{0,0},{8,1},{64,2},{72,3},{128,4},{136,5},{192,6},{200,7},{16,8},{... | collective-permute-start | bytes 110600 | tf_op jit(solution)/shard_map/ppermute | solution.py:282
Sparse Core Ops, SparseCore 0:
  55.0 26.3 all-gather.1
  106.2 26.6 reduce-scatter.4
  136.1 42.3 reduce-scatter.2

commit v5 on v4

--- a/solution.py
+++ b/solution.py
@@ -256,6 +256,16 @@
     return pairs
 
 
+def owner_pairs():
+    pairs = []
+    for a in range(8):
+        for x in range(4):
+            for z in range(8):
+                src = (((z // 2) * 4 + x) * 2 + z % 2) * 8 + a
+                pairs.append((src, ((a + 8 * (x // 2)) * 2 + x % 2) * 8 + z))
+    return pairs
+
+
 def body(query, key_proj, value, cotangent, out_weight):
     flip = [(0, 1), (1, 0)]
     a2a = functools.partial(lax.all_to_all, split_axis=0, concat_axis=0, tiled=True)
@@ -277,9 +287,9 @@
     out = backward(qkv, g_keep, g_recv, acc, after(lse, proj))
     projected = lax.psum_scatter(after(proj, out), YC, scatter_dimension=0, tiled=True)
     grads = a2a(out, SEQ)
-    parts = a2a(after(part, grads).astype(BF16).reshape(8, 6, WIDTH), Z8)
+    part = lax.ppermute(part.astype(BF16), ALL, owner_pairs())
+    parts = a2a(after(part, grads).reshape(8, 6, WIDTH), YC)
     grad_weight = jnp.sum(parts.astype(F32), axis=0)
-    grad_weight = lax.ppermute(grad_weight, ALL, [(d, s) for s, d in weight_pairs()])
 
     grad_query, grad_key, grad_value = back(grads)
     return (projected[None], grad_query[None], grad_key[None], grad_value[None], grad_weight)

time: 202 us -> 198 us (0.980)
  the two profiles are of different devices: /device:TPU:39 before, /device:TPU:4 now
where the time goes in v5:
time: 198 us
  starting transfers between devices  57.5 us (29%)
  blocking collectives  54.8 us (28%)
  Pallas kernels  39.1 us (20%)
  waiting for transfers between devices  27.5 us (14%)
  between operations  13.8 us (7%)
  local copies, waits for them, and re-layouts  3.3 us (2%)
    pallas_call x6, Pallas kernels, call(): pl.pallas_call(kernel, out_shape=tuple(outs), in_specs=specs, out_specs=t...  39.1 us
    all_to_all x1, blocking collectives, body(): qkv = a2a(prep(query[0], key_proj[0], value[0]), SEQ)  36.8 us
    all_to_all x1, starting transfers between devices, body(): parts = a2a(after(part, grads).reshape(8, 6, WIDTH), YC)  29.5 us
    all_to_all x1, blocking collectives, body(): w8 = a2a(after(jnp.broadcast_to(w_mine[None], (8, 6, WIDTH)), lse), Z8)  17.9 us
    all_to_all x1, waiting for transfers between devices, body(): grads = a2a(out, SEQ)  11.7 us
    all_to_all x1, starting transfers between devices, body(): grads = a2a(out, SEQ)  8.53 us
    all_to_all x1, starting transfers between devices, body(): a2a(jnp.broadcast_to(w8[None], (4, 8, 6, WIDTH)), 'x').reshape(32, 6, WIDTH)  6.35 us
    ppermute x1, starting transfers between devices, body(): part = lax.ppermute(part.astype(BF16), ALL, owner_pairs())  5.92 us
  transfers between devices with their start and end apart: 10, of which 6 were waited for; matrix products, arithmetic and copies ran while one was open for 2% of the time, Pallas kernels for 18%

profile of v5, /device:TPU:4, one launch (start us, length us, event | category | flops | bytes accessed | tf_op | source)
XLA Modules:
  0.0 197.6 jit_solution(4050605196358403407)
XLA Ops:
  7.2 2.6 %prep.1 = bf16[16,288,128]{2,1,0:T(8,128)(2,1)} custom-call(bf16[128,1536]{1,0:T(8,128)(2,1)} %bitcast.11, bf16[128,1536]{1,0:T(8,128)(2,1)} %bitcast.12, bf16[128,1536]{1,0:T(8,128)(2,1)} %bitcast.13), custom_call_target="tpu_custom_call" | custom-call | flops 1 | bytes 1 | tf_op jit(solution)/shard_map/prep/pallas_call | solution.py:37
  9.9 36.8 %all_to_all.25.qkv = bf16[16,288,128]{2,1,0:T(8,128)(2,1)} all-to-all(bf16[16,288,128]{2,1,0:T(8,128)(2,1)} %prep.1), channel_id=1, replica_groups=mesh['zl'=4,'x'=4,'zh'=2,'y'=4,'c'=2] {'zh','y','c'}, dimensions={0} | all-to-all | bytes 2359296 | tf_op jit(solution)/shard_map/all_to_all | solution.py:275
  46.7 1.9 collective-permute-start.1
  48.6 9.1 %fwd.1 = (bf16[8,96,128]{2,1,0:T(8,128)(2,1)}, bf16[8,96,128]{2,1,0:T(8,128)(2,1)}, f32[16,96,128]{2,1,0:T(8,128)}, f32[16,8,128]{2,1,0:T(8,128)}) custom-call(bf16[16,288,128]{2,1,0:T(8,128)(2,1)} %all_to_all.25.qkv, s32[1]{0:T(128)} %bitcast.3.side), custom_call_target="tpu_custom_call" | custom-call | flops 1 | bytes 1 | tf_op jit(solution)/shard_map/fwd/pallas_call | solution.py:37
  57.7 3.4 %collective-permute-done.1 = bf16[6,1536]{1,0:T(8,128)(2,1)S(1)} collective-permute-done((bf16[6,1536]{1,0:T(8,128)(2,1)S(1)}, bf16[6,1536]{1,0:T(8,128)(2,1)S(1)}, u32[]{:S(2)}, u32[]{:S(2)}) %collective-permute-start.1) | collective-permute-done | bytes 18464 | tf_op jit(solution)/shard_map/ppermute | solution.py:276
  61.1 17.9 %all_to_all.26 = bf16[8,6,1536]{2,1,0:T(8,128)(2,1)S(1)} all-to-all(bf16[8,6,1536]{2,1,0:T(8,128)(2,1)S(1)} %broadcast_in_dim.24), channel_id=1, replica_groups=mesh['zl'=4,'x'=4,'zh'=2,'y'=4,'c'=2] {'zl','zh'}, dimensions={0} | all-to-all | bytes 294912 | tf_op jit(solution)/shard_map/all_to_all | solution.py:279
  79.1 0.9 broadcast_in_dim.25
  80.0 6.3 %all-to-all-start.2 = ((bf16[4,8,6,1536]{3,1,2,0:T(8,128)(2,1)}), bf16[4,8,6,1536]{3,1,2,0:T(8,128)(2,1)S(1)}, u32[]{:S(2)}, u32[]{:S(2)}) async-start(bf16[4,8,6,1536]{3,1,2,0:T(8,128)(2,1)} %broadcast_in_dim.25), calls=%async_computation.2 | async-start | bytes 1179648 | tf_op jit(solution)/shard_map/all_to_all | solution.py:282
  86.3 2.3 %collective-permute-start = (bf16[8,96,128]{2,1,0:T(8,128)(2,1)S(1)}, bf16[8,96,128]{2,1,0:T(8,128)(2,1)S(1)}, u32[]{:S(2)}, u32[]{:S(2)}) collective-permute-start(bf16[8,96,128]{2,1,0:T(8,128)(2,1)S(1)} %copy-done.3), channel_id=1, source_target_pairs={{0,8},{8,0},{1,9},{9,1},{2,10},{10,2},{3,11},{11,3},{4,12},{12,4},... | collective-permute-start | bytes 589832 | tf_op jit(solution)/shard_map/ppermute | solution.py:272
  88.6 3.1 %all-to-all-done.2 = bf16[4,8,6,1536]{3,1,2,0:T(8,128)(2,1)S(1)} async-done(((bf16[4,8,6,1536]{3,1,2,0:T(8,128)(2,1)}), bf16[4,8,6,1536]{3,1,2,0:T(8,128)(2,1)S(1)}, u32[]{:S(2)}, u32[]{:S(2)}) %all-to-all-start.2) | async-done | bytes 589856 | tf_op jit(solution)/shard_map/all_to_all | solution.py:282
  91.8 1.1 copy.12
  92.9 4.4 %grad_att.1 = (bf16[192,1536]{1,0:T(8,128)(2,1)}, bf16[8,96,128]{2,1,0:T(8,128)(2,1)}, bf16[8,96,128]{2,1,0:T(8,128)(2,1)}) custom-call(bf16[32,6,1536]{2,1,0:T(8,128)(2,1)} %bitcast.10, bf16[1024,1536]{1,0:T(8,128)(2,1)} %all-gather.2.cloned.1.call-done.cot, s32[1]{0:T(128)} %bitcast.3.side), custom_call_target="tpu_custom_call" | custom-call | flops 1 | bytes 1 | tf_op jit(solution)/shard_map/grad_att/pallas_call | solution.py:37
  97.3 2.6 %collective-permute-start.2 = (bf16[8,96,128]{2,1,0:T(8,128)(2,1)}, bf16[8,96,128]{2,1,0:T(8,128)(2,1)S(1)}, u32[]{:S(2)}, u32[]{:S(2)}) collective-permute-start(bf16[8,96,128]{2,1,0:T(8,128)(2,1)} %get-tuple-element.37), channel_id=1, source_target_pairs={{0,8},{8,0},{1,9},{9,1},{2,10},{10,2},{3,11},{11,3},{4,12},{12,4},... | collective-permute-start | bytes 589832 | tf_op jit(solution)/shard_map/ppermute | solution.py:272
  99.9 6.4 %grad_w.1 = (f32[192,1536]{1,0:T(8,128)}, bf16[1024,1536]{1,0:T(8,128)(2,1)}) custom-call(bf16[8,96,128]{2,1,0:T(8,128)(2,1)} %get-tuple-element.26.keep, bf16[8,96,128]{2,1,0:T(8,128)(2,1)} %copy-done.1, bf16[1024,1536]{1,0:T(8,128)(2,1)} %all-gather.2.cloned.1.call-done.cot, bf16[192,1536]{1,0:T(8,128)(2,1)} %get-tuple-element.33.w_pair, s32[1]{0:T(128)} %bitcast.3.side), custom_call_target="tpu_custom_call" | custom-call | flops 1 | bytes 1 | tf_op jit(solution)/shard_map/grad_w/pallas_call | solution.py:37
  106.3 1.5 collective-permute-done.2.recv
  108.5 14.2 %bwd.1 = bf16[16,288,128]{2,1,0:T(8,128)(2,1)} custom-call(bf16[16,288,128]{2,1,0:T(8,128)(2,1)} %all_to_all.25.qkv, bf16[8,96,128]{2,1,0:T(8,128)(2,1)} %get-tuple-element.35.keep, bf16[8,96,128]{2,1,0:T(8,128)(2,1)} %copy-done.2, f32[16,96,128]{2,1,0:T(8,128)} %get-tuple-element.38.acc_in, f32[16,8,128]{2,1,0:T(8,128)} %get-tuple-element.39.lse_in, ...), custom_call_target="tpu_custom_call" | custom-call | flops 1 | bytes 1 | tf_op jit(solution)/shard_map/bwd/pallas_call | solution.py:37
  122.7 8.5 %all-to-all-start.3 = ((bf16[16,288,128]{2,1,0:T(8,128)(2,1)}), bf16[16,288,128]{2,1,0:T(8,128)(2,1)S(1)}, u32[]{:S(2)}, u32[]{:S(2)}) async-start(bf16[16,288,128]{2,1,0:T(8,128)(2,1)} %bwd.1), calls=%async_computation.4 | async-start | bytes 2359296 | tf_op jit(solution)/shard_map/all_to_all | solution.py:289
  131.3 3.4 %reduce-scatter.5.cloned.1.call-done = f32[48,1536]{1,0:T(8,128)} async-done(((f32[192,1536]{1,0:T(8,128)}), f32[48,1536]{1,0:T(8,128)}) %reduce-scatter.5.cloned.1.call-update) | async-done | bytes 294928 | tf_op jit(solution)/shard_map/reduce_scatter | solution.py:286
  134.7 1.0 convert_element_type.6
  135.6 5.9 %collective-permute-start.3 = (bf16[48,1536]{1,0:T(8,128)(2,1)S(1)}, bf16[48,1536]{1,0:T(8,128)(2,1)S(1)}, u32[]{:S(2)}, u32[]{:S(2)}) collective-permute-start(bf16[48,1536]{1,0:T(8,128)(2,1)S(1)} %convert_element_type.6), channel_id=1, source_target_pairs={{0,0},{8,1},{64,2},{72,3},{128,4},{136,5},{192,6},{200,7},{16,8},{... | collective-permute-start | bytes 442376 | tf_op jit(solution)/shard_map/ppermute | solution.py:290
  141.6 11.7 %all-to-all-done.3.src = bf16[16,288,128]{2,1,0:T(8,128)(2,1)S(1)} async-done(((bf16[16,288,128]{2,1,0:T(8,128)(2,1)}), bf16[16,288,128]{2,1,0:T(8,128)(2,1)S(1)}, u32[]{:S(2)}, u32[]{:S(2)}) %all-to-all-start.3) | async-done | bytes 1179680 | tf_op jit(solution)/shard_map/all_to_all | solution.py:289
  154.0 29.5 %all-to-all-start.4 = ((bf16[8,6,1536]{2,1,0:T(8,128)(2,1)}), bf16[8,6,1536]{2,1,0:T(8,128)(2,1)S(1)}, u32[]{:S(2)}, u32[]{:S(2)}) async-start(bf16[8,6,1536]{2,1,0:T(8,128)(2,1)} %reshape.26), calls=%async_computation.6 | async-start | bytes 393216 | tf_op jit(solution)/shard_map/all_to_all | solution.py:291
  183.6 2.4 %back.1 = (bf16[128,1536]{1,0:T(8,128)(2,1)}, bf16[128,1536]{1,0:T(8,128)(2,1)}, bf16[128,1536]{1,0:T(8,128)(2,1)}) custom-call(bf16[16,288,128]{2,1,0:T(8,128)(2,1)} %copy-done), custom_call_target="tpu_custom_call" | custom-call | flops 1 | bytes 1 | tf_op jit(solution)/shard_map/back/pallas_call | solution.py:37
  186.0 4.4 %all-to-all-done.4 = bf16[8,6,1536]{2,1,0:T(8,128)(2,1)S(1)} async-done(((bf16[8,6,1536]{2,1,0:T(8,128)(2,1)}), bf16[8,6,1536]{2,1,0:T(8,128)(2,1)S(1)}, u32[]{:S(2)}, u32[]{:S(2)}) %all-to-all-start.4) | async-done | bytes 147488 | tf_op jit(solution)/shard_map/all_to_all | solution.py:291
  (24 shorter events, 2.3 us)
Async XLA Ops:
  7.2 85.7 %all-gather.2.cloned.1.call-start = ((), (), s32[]{:S(2)}) async-start(), calls=%async_computation.7 | async-start | bytes 3538944 | tf_op jit(solution)/shard_map/all_gather | solution.py:277
  9.9 36.8 %copy-start.4 = (bf16[6,1536]{1,0:T(8,128)(2,1)S(1)}, bf16[6,1536]{1,0:T(8,128)(2,1)}, u32[]{:S(2)}) copy-start(bf16[6,1536]{1,0:T(8,128)(2,1)} %param.9) | copy-start | bytes 55300
  46.7 14.4 %collective-permute-start.1 = (bf16[6,1536]{1,0:T(8,128)(2,1)S(1)}, bf16[6,1536]{1,0:T(8,128)(2,1)S(1)}, u32[]{:S(2)}, u32[]{:S(2)}) collective-permute-start(bf16[6,1536]{1,0:T(8,128)(2,1)S(1)} %copy-done.4), channel_id=1, source_target_pairs={{0,0},{1,8},{2,64},{3,72},{4,128},{5,136},{6,192},{7,200},{8,16},{... | collective-permute-start | bytes 55304 | tf_op jit(solution)/shard_map/ppermute | solution.py:276
  79.0 7.3 %copy-start.3 = (bf16[8,96,128]{2,1,0:T(8,128)(2,1)S(1)}, bf16[8,96,128]{2,1,0:T(8,128)(2,1)}, u32[]{:S(2)}) copy-start(bf16[8,96,128]{2,1,0:T(8,128)(2,1)} %get-tuple-element.27) | copy-start | bytes 589828
  80.0 11.8 %all-to-all-start.2 = ((bf16[4,8,6,1536]{3,1,2,0:T(8,128)(2,1)}), bf16[4,8,6,1536]{3,1,2,0:T(8,128)(2,1)S(1)}, u32[]{:S(2)}, u32[]{:S(2)}) async-start(bf16[4,8,6,1536]{3,1,2,0:T(8,128)(2,1)} %broadcast_in_dim.25), calls=%async_computation.2 | async-start | bytes 1179648 | tf_op jit(solution)/shard_map/all_to_all | solution.py:282
  86.3 48.3 %reduce-scatter.5.cloned.1.call-start = ((), (), s32[]{:S(2)}) async-start(), calls=%async_computation.9 | async-start | bytes 1474560 | tf_op jit(solution)/shard_map/reduce_scatter | solution.py:286
  86.3 11.0 %collective-permute-start = (bf16[8,96,128]{2,1,0:T(8,128)(2,1)S(1)}, bf16[8,96,128]{2,1,0:T(8,128)(2,1)S(1)}, u32[]{:S(2)}, u32[]{:S(2)}) collective-permute-start(bf16[8,96,128]{2,1,0:T(8,128)(2,1)S(1)} %copy-done.3), channel_id=1, source_target_pairs={{0,8},{8,0},{1,9},{9,1},{2,10},{10,2},{3,11},{11,3},{4,12},{12,4},... | collective-permute-start | bytes 589832 | tf_op jit(solution)/shard_map/ppermute | solution.py:272
  97.3 2.6 %copy-start.1 = (bf16[8,96,128]{2,1,0:T(8,128)(2,1)}, bf16[8,96,128]{2,1,0:T(8,128)(2,1)S(1)}, u32[]{:S(2)}) copy-start(bf16[8,96,128]{2,1,0:T(8,128)(2,1)S(1)} %collective-permute-done.recv) | copy-start | bytes 589828
  97.3 10.5 %collective-permute-start.2 = (bf16[8,96,128]{2,1,0:T(8,128)(2,1)}, bf16[8,96,128]{2,1,0:T(8,128)(2,1)S(1)}, u32[]{:S(2)}, u32[]{:S(2)}) collective-permute-start(bf16[8,96,128]{2,1,0:T(8,128)(2,1)} %get-tuple-element.37), channel_id=1, source_target_pairs={{0,8},{8,0},{1,9},{9,1},{2,10},{10,2},{3,11},{11,3},{4,12},{12,4},... | collective-permute-start | bytes 589832 | tf_op jit(solution)/shard_map/ppermute | solution.py:272
  107.8 0.7 copy-start.2
  107.8 83.3 %reduce-scatter.3.cloned.1.call-start = ((), (), s32[]{:S(2)}) async-start(), calls=%async_computation.8 | async-start | bytes 3538944 | tf_op jit(solution)/shard_map/reduce_scatter | solution.py:288
  122.7 30.5 %all-to-all-start.3 = ((bf16[16,288,128]{2,1,0:T(8,128)(2,1)}), bf16[16,288,128]{2,1,0:T(8,128)(2,1)S(1)}, u32[]{:S(2)}, u32[]{:S(2)}) async-start(bf16[16,288,128]{2,1,0:T(8,128)(2,1)} %bwd.1), calls=%async_computation.4 | async-start | bytes 2359296 | tf_op jit(solution)/shard_map/all_to_all | solution.py:289
  135.6 17.6 %collective-permute-start.3 = (bf16[48,1536]{1,0:T(8,128)(2,1)S(1)}, bf16[48,1536]{1,0:T(8,128)(2,1)S(1)}, u32[]{:S(2)}, u32[]{:S(2)}) collective-permute-start(bf16[48,1536]{1,0:T(8,128)(2,1)S(1)} %convert_element_type.6), channel_id=1, source_target_pairs={{0,0},{8,1},{64,2},{72,3},{128,4},{136,5},{192,6},{200,7},{16,8},{... | collective-permute-start | bytes 442376 | tf_op jit(solution)/shard_map/ppermute | solution.py:290
  153.2 30.3 %copy-start = (bf16[16,288,128]{2,1,0:T(8,128)(2,1)}, bf16[16,288,128]{2,1,0:T(8,128)(2,1)S(1)}, u32[]{:S(2)}) copy-start(bf16[16,288,128]{2,1,0:T(8,128)(2,1)S(1)} %all-to-all-done.3.src) | copy-start | bytes 3538948
  154.0 36.4 %all-to-all-start.4 = ((bf16[8,6,1536]{2,1,0:T(8,128)(2,1)}), bf16[8,6,1536]{2,1,0:T(8,128)(2,1)S(1)}, u32[]{:S(2)}, u32[]{:S(2)}) async-start(bf16[8,6,1536]{2,1,0:T(8,128)(2,1)} %reshape.26), calls=%async_computation.6 | async-start | bytes 393216 | tf_op jit(solution)/shard_map/all_to_all | solution.py:291
Sparse Core Ops, SparseCore 0:
  46.8 34.4 all-gather.1
  107.9 26.6 reduce-scatter.4
  137.8 40.1 reduce-scatter.2

commit v6 on v5

--- a/solution.py
+++ b/solution.py
@@ -25,7 +25,6 @@
 ALL = ("zl", "x", "zh", "y", "c")
 SEQ = ("zh", "y", "c")
 YC = ("y", "c")
-Z8 = ("zl", "zh")
 
 
 def call(kernel, ins, outs, scratch=(), side=False, us=1, name=None):
@@ -246,16 +245,6 @@
     )
 
 
-def weight_pairs():
-    pairs = []
-    for a in range(8):
-        for n in range(32):
-            b, s = divmod(n, 16)
-            x, zl, zh = n // 8, n % 8 // 2, n % 2
-            pairs.append(((a + 8 * b) * 16 + s, ((zl * 4 + x) * 2 + zh) * 8 + a))
-    return pairs
-
-
 def owner_pairs():
     pairs = []
     for a in range(8):
@@ -272,11 +261,11 @@
     swap = lambda x: lax.ppermute(x, "zh", flip)
     after = lambda x, *others: lax.optimization_barrier((x, *others))[0]
 
-    qkv = a2a(prep(query[0], key_proj[0], value[0]), SEQ)
-    w_mine = lax.ppermute(after(out_weight, qkv), ALL, weight_pairs())
+    w8 = a2a(jnp.broadcast_to(out_weight[None], (8, 6, WIDTH)), YC)
+    qkv = a2a(after(prep(query[0], key_proj[0], value[0]), w8), SEQ)
+    w8 = lax.ppermute(after(w8, qkv), ALL, [(d, s) for s, d in owner_pairs()])
     cot = lax.all_gather(after(cotangent[0], qkv), YC, axis=0, tiled=True)
     att_keep, att_send, acc, lse = forward(qkv)
-    w8 = a2a(after(jnp.broadcast_to(w_mine[None], (8, 6, WIDTH)), lse), Z8)
     att_recv = swap(att_send)
     w8 = after(w8, lse)
     w32 = a2a(jnp.broadcast_to(w8[None], (4, 8, 6, WIDTH)), "x").reshape(32, 6, WIDTH)

time: 198 us -> 195 us (0.985)
  the two profiles are of different devices: /device:TPU:4 before, /device:TPU:39 now
where the time goes in v6:
time: 195 us; the launch traced here: 192 us
  waiting for transfers between devices  50 us (26%)
  blocking collectives  43.2 us (22%)
  starting transfers between devices  39.6 us (20%)
  Pallas kernels  39.2 us (20%)
  between operations  13.8 us (7%)
  local copies, waits for them, and re-layouts  4.67 us (2%)
    all_to_all x1, blocking collectives, body(): qkv = a2a(after(prep(query[0], key_proj[0], value[0]), w8), SEQ)  43.2 us
    pallas_call x6, Pallas kernels, call(): pl.pallas_call(kernel, out_shape=tuple(outs), in_specs=specs, out_specs=t...  39.2 us
    all_to_all x1, waiting for transfers between devices, body(): grads = a2a(out, SEQ)  20.3 us
    ppermute x1, waiting for transfers between devices, body(): part = lax.ppermute(part.astype(BF16), ALL, owner_pairs())  9.84 us
    ppermute x1, starting transfers between devices, body(): part = lax.ppermute(part.astype(BF16), ALL, owner_pairs())  8.79 us
    all_to_all x1, starting transfers between devices, body(): grads = a2a(out, SEQ)  8.61 us
    ppermute x1, waiting for transfers between devices, body(): w8 = lax.ppermute(after(w8, qkv), ALL, [(d, s) for s, d in owner_pairs()])  7.35 us
    ppermute x2, starting transfers between devices, body(): swap = lambda x: lax.ppermute(x, 'zh', flip)  6.03 us
  transfers between devices with their start and end apart: 11, of which 8 were waited for; matrix products, arithmetic and copies ran while one was open for 2% of the time, Pallas kernels for 20%

profile of v6, /device:TPU:39, one launch (start us, length us, event | category | flops | bytes accessed | tf_op | source)
XLA Modules:
  0.0 192.0 jit_solution(10940371711606215166)
XLA Ops:
  7.2 1.4 broadcast_in_dim.24
  8.6 5.1 %all-to-all-start = ((bf16[8,6,1536]{2,1,0:T(8,128)(2,1)}), bf16[8,6,1536]{2,1,0:T(8,128)(2,1)S(1)}, u32[]{:S(2)}, u32[]{:S(2)}) async-start(bf16[8,6,1536]{2,1,0:T(8,128)(2,1)} %broadcast_in_dim.24), calls=%async_computation | async-start | bytes 393216 | tf_op jit(solution)/shard_map/all_to_all | solution.py:264
  13.7 2.6 %prep.1 = bf16[16,288,128]{2,1,0:T(8,128)(2,1)} custom-call(bf16[128,1536]{1,0:T(8,128)(2,1)} %bitcast.11, bf16[128,1536]{1,0:T(8,128)(2,1)} %bitcast.12, bf16[128,1536]{1,0:T(8,128)(2,1)} %bitcast.13), custom_call_target="tpu_custom_call" | custom-call | flops 1 | bytes 1 | tf_op jit(solution)/shard_map/prep/pallas_call | solution.py:36
  16.4 3.3 %all-to-all-done = bf16[8,6,1536]{2,1,0:T(8,128)(2,1)S(1)} async-done(((bf16[8,6,1536]{2,1,0:T(8,128)(2,1)}), bf16[8,6,1536]{2,1,0:T(8,128)(2,1)S(1)}, u32[]{:S(2)}, u32[]{:S(2)}) %all-to-all-start) | async-done | bytes 147488 | tf_op jit(solution)/shard_map/all_to_all | solution.py:264
  19.6 43.2 %all_to_all.25.qkv = bf16[16,288,128]{2,1,0:T(8,128)(2,1)} all-to-all(bf16[16,288,128]{2,1,0:T(8,128)(2,1)} %prep.1), channel_id=1, replica_groups=mesh['zl'=4,'x'=4,'zh'=2,'y'=4,'c'=2] {'zh','y','c'}, dimensions={0} | all-to-all | bytes 2359296 | tf_op jit(solution)/shard_map/all_to_all | solution.py:265
  62.8 1.9 %collective-permute-start.1 = (bf16[8,6,1536]{2,1,0:T(8,128)(2,1)S(1)}, bf16[8,6,1536]{2,1,0:T(8,128)(2,1)S(1)}, u32[]{:S(2)}, u32[]{:S(2)}) collective-permute-start(bf16[8,6,1536]{2,1,0:T(8,128)(2,1)S(1)} %all-to-all-done), channel_id=1, source_target_pairs={{0,0},{1,8},{2,64},{3,72},{4,128},{5,136},{6,192},{7,200},{8,16},{... | collective-permute-start | bytes 442376 | tf_op jit(solution)/shard_map/ppermute | solution.py:266
  64.7 9.1 %fwd.1 = (bf16[8,96,128]{2,1,0:T(8,128)(2,1)}, bf16[8,96,128]{2,1,0:T(8,128)(2,1)}, f32[16,96,128]{2,1,0:T(8,128)}, f32[16,8,128]{2,1,0:T(8,128)}) custom-call(bf16[16,288,128]{2,1,0:T(8,128)(2,1)} %all_to_all.25.qkv, s32[1]{0:T(128)} %bitcast.3.side), custom_call_target="tpu_custom_call" | custom-call | flops 1 | bytes 1 | tf_op jit(solution)/shard_map/fwd/pallas_call | solution.py:36
  73.8 7.4 %collective-permute-done.1 = bf16[8,6,1536]{2,1,0:T(8,128)(2,1)S(1)} collective-permute-done((bf16[8,6,1536]{2,1,0:T(8,128)(2,1)S(1)}, bf16[8,6,1536]{2,1,0:T(8,128)(2,1)S(1)}, u32[]{:S(2)}, u32[]{:S(2)}) %collective-permute-start.1) | collective-permute-done | bytes 147488 | tf_op jit(solution)/shard_map/ppermute | solution.py:266
  82.1 3.9 %all-to-all-start.2 = ((bf16[4,8,6,1536]{3,1,2,0:T(8,128)(2,1)}), bf16[4,8,6,1536]{3,1,2,0:T(8,128)(2,1)S(1)}, u32[]{:S(2)}, u32[]{:S(2)}) async-start(bf16[4,8,6,1536]{3,1,2,0:T(8,128)(2,1)} %broadcast_in_dim.25), calls=%async_computation.2 | async-start | bytes 1179648 | tf_op jit(solution)/shard_map/all_to_all | solution.py:271
  86.0 3.0 %collective-permute-start = (bf16[8,96,128]{2,1,0:T(8,128)(2,1)S(1)}, bf16[8,96,128]{2,1,0:T(8,128)(2,1)S(1)}, u32[]{:S(2)}, u32[]{:S(2)}) collective-permute-start(bf16[8,96,128]{2,1,0:T(8,128)(2,1)S(1)} %copy-done.3), channel_id=1, source_target_pairs={{0,8},{8,0},{1,9},{9,1},{2,10},{10,2},{3,11},{11,3},{4,12},{12,4},... | collective-permute-start | bytes 589832 | tf_op jit(solution)/shard_map/ppermute | solution.py:261
  89.1 2.9 %all-to-all-done.2 = bf16[4,8,6,1536]{3,1,2,0:T(8,128)(2,1)S(1)} async-done(((bf16[4,8,6,1536]{3,1,2,0:T(8,128)(2,1)}), bf16[4,8,6,1536]{3,1,2,0:T(8,128)(2,1)S(1)}, u32[]{:S(2)}, u32[]{:S(2)}) %all-to-all-start.2) | async-done | bytes 589856 | tf_op jit(solution)/shard_map/all_to_all | solution.py:271
  92.0 1.1 copy.12
  93.1 2.6 %all-gather.2.cloned.1.call-done.cot = bf16[1024,1536]{1,0:T(8,128)(2,1)} async-done(((bf16[128,1536]{1,0:T(8,128)(2,1)}), bf16[1024,1536]{1,0:T(8,128)(2,1)}) %all-gather.2.cloned.1.call-update) | async-done | bytes 3145744 | tf_op jit(solution)/shard_map/all_gather | solution.py:267
  95.7 4.4 %grad_att.1 = (bf16[192,1536]{1,0:T(8,128)(2,1)}, bf16[8,96,128]{2,1,0:T(8,128)(2,1)}, bf16[8,96,128]{2,1,0:T(8,128)(2,1)}) custom-call(bf16[32,6,1536]{2,1,0:T(8,128)(2,1)} %bitcast.10, bf16[1024,1536]{1,0:T(8,128)(2,1)} %all-gather.2.cloned.1.call-done.cot, s32[1]{0:T(128)} %bitcast.3.side), custom_call_target="tpu_custom_call" | custom-call | flops 1 | bytes 1 | tf_op jit(solution)/shard_map/grad_att/pallas_call | solution.py:36
  100.1 3.0 %collective-permute-start.2 = (bf16[8,96,128]{2,1,0:T(8,128)(2,1)}, bf16[8,96,128]{2,1,0:T(8,128)(2,1)S(1)}, u32[]{:S(2)}, u32[]{:S(2)}) collective-permute-start(bf16[8,96,128]{2,1,0:T(8,128)(2,1)} %get-tuple-element.37), channel_id=1, source_target_pairs={{0,8},{8,0},{1,9},{9,1},{2,10},{10,2},{3,11},{11,3},{4,12},{12,4},... | collective-permute-start | bytes 589832 | tf_op jit(solution)/shard_map/ppermute | solution.py:261
  103.1 6.4 %grad_w.1 = (f32[192,1536]{1,0:T(8,128)}, bf16[1024,1536]{1,0:T(8,128)(2,1)}) custom-call(bf16[8,96,128]{2,1,0:T(8,128)(2,1)} %get-tuple-element.27.keep, bf16[8,96,128]{2,1,0:T(8,128)(2,1)} %copy-done.1, bf16[1024,1536]{1,0:T(8,128)(2,1)} %all-gather.2.cloned.1.call-done.cot, bf16[192,1536]{1,0:T(8,128)(2,1)} %get-tuple-element.33.w_pair, s32[1]{0:T(128)} %bitcast.3.side), custom_call_target="tpu_custom_call" | custom-call | flops 1 | bytes 1 | tf_op jit(solution)/shard_map/grad_w/pallas_call | solution.py:36
  110.5 14.2 %bwd.1 = bf16[16,288,128]{2,1,0:T(8,128)(2,1)} custom-call(bf16[16,288,128]{2,1,0:T(8,128)(2,1)} %all_to_all.25.qkv, bf16[8,96,128]{2,1,0:T(8,128)(2,1)} %get-tuple-element.35.keep, bf16[8,96,128]{2,1,0:T(8,128)(2,1)} %copy-done.2, f32[16,96,128]{2,1,0:T(8,128)} %get-tuple-element.38.acc_in, f32[16,8,128]{2,1,0:T(8,128)} %get-tuple-element.39.lse_in, ...), custom_call_target="tpu_custom_call" | custom-call | flops 1 | bytes 1 | tf_op jit(solution)/shard_map/bwd/pallas_call | solution.py:36
  124.7 8.6 %all-to-all-start.3 = ((bf16[16,288,128]{2,1,0:T(8,128)(2,1)}), bf16[16,288,128]{2,1,0:T(8,128)(2,1)S(1)}, u32[]{:S(2)}, u32[]{:S(2)}) async-start(bf16[16,288,128]{2,1,0:T(8,128)(2,1)} %bwd.1), calls=%async_computation.4 | async-start | bytes 2359296 | tf_op jit(solution)/shard_map/all_to_all | solution.py:278
  134.3 8.8 %collective-permute-start.3 = (bf16[48,1536]{1,0:T(8,128)(2,1)S(1)}, bf16[48,1536]{1,0:T(8,128)(2,1)S(1)}, u32[]{:S(2)}, u32[]{:S(2)}) collective-permute-start(bf16[48,1536]{1,0:T(8,128)(2,1)S(1)} %convert_element_type.6), channel_id=1, source_target_pairs={{0,0},{8,1},{64,2},{72,3},{128,4},{136,5},{192,6},{200,7},{16,8},{... | collective-permute-start | bytes 442376 | tf_op jit(solution)/shard_map/ppermute | solution.py:279
  143.1 20.3 %all-to-all-done.3.src = bf16[16,288,128]{2,1,0:T(8,128)(2,1)S(1)} async-done(((bf16[16,288,128]{2,1,0:T(8,128)(2,1)}), bf16[16,288,128]{2,1,0:T(8,128)(2,1)S(1)}, u32[]{:S(2)}, u32[]{:S(2)}) %all-to-all-start.3) | async-done | bytes 1179680 | tf_op jit(solution)/shard_map/all_to_all | solution.py:278
  163.4 9.8 %collective-permute-done.3 = bf16[48,1536]{1,0:T(8,128)(2,1)S(1)} collective-permute-done((bf16[48,1536]{1,0:T(8,128)(2,1)S(1)}, bf16[48,1536]{1,0:T(8,128)(2,1)S(1)}, u32[]{:S(2)}, u32[]{:S(2)}) %collective-permute-start.3) | collective-permute-done | bytes 147488 | tf_op jit(solution)/shard_map/ppermute | solution.py:279
  174.0 4.9 %all-to-all-start.4 = ((bf16[8,6,1536]{2,1,0:T(8,128)(2,1)}), bf16[8,6,1536]{2,1,0:T(8,128)(2,1)S(1)}, u32[]{:S(2)}, u32[]{:S(2)}) async-start(bf16[8,6,1536]{2,1,0:T(8,128)(2,1)} %reshape.26), calls=%async_computation.6 | async-start | bytes 393216 | tf_op jit(solution)/shard_map/all_to_all | solution.py:280
  178.9 2.4 %back.1 = (bf16[128,1536]{1,0:T(8,128)(2,1)}, bf16[128,1536]{1,0:T(8,128)(2,1)}, bf16[128,1536]{1,0:T(8,128)(2,1)}) custom-call(bf16[16,288,128]{2,1,0:T(8,128)(2,1)} %copy-done), custom_call_target="tpu_custom_call" | custom-call | flops 1 | bytes 1 | tf_op jit(solution)/shard_map/back/pallas_call | solution.py:36
  181.4 3.5 %all-to-all-done.4 = bf16[8,6,1536]{2,1,0:T(8,128)(2,1)S(1)} async-done(((bf16[8,6,1536]{2,1,0:T(8,128)(2,1)}), bf16[8,6,1536]{2,1,0:T(8,128)(2,1)S(1)}, u32[]{:S(2)}, u32[]{:S(2)}) %all-to-all-start.4) | async-done | bytes 147488 | tf_op jit(solution)/shard_map/all_to_all | solution.py:280
  (23 shorter events, 4.3 us)
Async XLA Ops:
  8.6 11.0 %all-to-all-start = ((bf16[8,6,1536]{2,1,0:T(8,128)(2,1)}), bf16[8,6,1536]{2,1,0:T(8,128)(2,1)S(1)}, u32[]{:S(2)}, u32[]{:S(2)}) async-start(bf16[8,6,1536]{2,1,0:T(8,128)(2,1)} %broadcast_in_dim.24), calls=%async_computation | async-start | bytes 393216 | tf_op jit(solution)/shard_map/all_to_all | solution.py:264
  13.7 82.0 %all-gather.2.cloned.1.call-start = ((), (), s32[]{:S(2)}) async-start(), calls=%async_computation.7 | async-start | bytes 3538944 | tf_op jit(solution)/shard_map/all_gather | solution.py:267
  62.8 18.3 %collective-permute-start.1 = (bf16[8,6,1536]{2,1,0:T(8,128)(2,1)S(1)}, bf16[8,6,1536]{2,1,0:T(8,128)(2,1)S(1)}, u32[]{:S(2)}, u32[]{:S(2)}) collective-permute-start(bf16[8,6,1536]{2,1,0:T(8,128)(2,1)S(1)} %all-to-all-done), channel_id=1, source_target_pairs={{0,0},{1,8},{2,64},{3,72},{4,128},{5,136},{6,192},{7,200},{8,16},{... | collective-permute-start | bytes 442376 | tf_op jit(solution)/shard_map/ppermute | solution.py:266
  73.8 12.2 %copy-start.3 = (bf16[8,96,128]{2,1,0:T(8,128)(2,1)S(1)}, bf16[8,96,128]{2,1,0:T(8,128)(2,1)}, u32[]{:S(2)}) copy-start(bf16[8,96,128]{2,1,0:T(8,128)(2,1)} %get-tuple-element.28) | copy-start | bytes 589828
  82.1 9.9 %all-to-all-start.2 = ((bf16[4,8,6,1536]{3,1,2,0:T(8,128)(2,1)}), bf16[4,8,6,1536]{3,1,2,0:T(8,128)(2,1)S(1)}, u32[]{:S(2)}, u32[]{:S(2)}) async-start(bf16[4,8,6,1536]{3,1,2,0:T(8,128)(2,1)} %broadcast_in_dim.25), calls=%async_computation.2 | async-start | bytes 1179648 | tf_op jit(solution)/shard_map/all_to_all | solution.py:271
  86.0 47.3 %reduce-scatter.5.cloned.1.call-start = ((), (), s32[]{:S(2)}) async-start(), calls=%async_computation.9 | async-start | bytes 1474560 | tf_op jit(solution)/shard_map/reduce_scatter | solution.py:275
  86.0 14.0 %collective-permute-start = (bf16[8,96,128]{2,1,0:T(8,128)(2,1)S(1)}, bf16[8,96,128]{2,1,0:T(8,128)(2,1)S(1)}, u32[]{:S(2)}, u32[]{:S(2)}) collective-permute-start(bf16[8,96,128]{2,1,0:T(8,128)(2,1)S(1)} %copy-done.3), channel_id=1, source_target_pairs={{0,8},{8,0},{1,9},{9,1},{2,10},{10,2},{3,11},{11,3},{4,12},{12,4},... | collective-permute-start | bytes 589832 | tf_op jit(solution)/shard_map/ppermute | solution.py:261
  100.1 3.0 %copy-start.1 = (bf16[8,96,128]{2,1,0:T(8,128)(2,1)}, bf16[8,96,128]{2,1,0:T(8,128)(2,1)S(1)}, u32[]{:S(2)}) copy-start(bf16[8,96,128]{2,1,0:T(8,128)(2,1)S(1)} %collective-permute-done.recv) | copy-start | bytes 589828
  100.1 9.7 %collective-permute-start.2 = (bf16[8,96,128]{2,1,0:T(8,128)(2,1)}, bf16[8,96,128]{2,1,0:T(8,128)(2,1)S(1)}, u32[]{:S(2)}, u32[]{:S(2)}) collective-permute-start(bf16[8,96,128]{2,1,0:T(8,128)(2,1)} %get-tuple-element.37), channel_id=1, source_target_pairs={{0,8},{8,0},{1,9},{9,1},{2,10},{10,2},{3,11},{11,3},{4,12},{12,4},... | collective-permute-start | bytes 589832 | tf_op jit(solution)/shard_map/ppermute | solution.py:261
  109.8 0.7 copy-start.2
  109.8 75.7 %reduce-scatter.3.cloned.1.call-start = ((), (), s32[]{:S(2)}) async-start(), calls=%async_computation.8 | async-start | bytes 3538944 | tf_op jit(solution)/shard_map/reduce_scatter | solution.py:277
  124.7 38.7 %all-to-all-start.3 = ((bf16[16,288,128]{2,1,0:T(8,128)(2,1)}), bf16[16,288,128]{2,1,0:T(8,128)(2,1)S(1)}, u32[]{:S(2)}, u32[]{:S(2)}) async-start(bf16[16,288,128]{2,1,0:T(8,128)(2,1)} %bwd.1), calls=%async_computation.4 | async-start | bytes 2359296 | tf_op jit(solution)/shard_map/all_to_all | solution.py:278
  134.3 38.9 %collective-permute-start.3 = (bf16[48,1536]{1,0:T(8,128)(2,1)S(1)}, bf16[48,1536]{1,0:T(8,128)(2,1)S(1)}, u32[]{:S(2)}, u32[]{:S(2)}) collective-permute-start(bf16[48,1536]{1,0:T(8,128)(2,1)S(1)} %convert_element_type.6), channel_id=1, source_target_pairs={{0,0},{8,1},{64,2},{72,3},{128,4},{136,5},{192,6},{200,7},{16,8},{... | collective-permute-start | bytes 442376 | tf_op jit(solution)/shard_map/ppermute | solution.py:279
  163.4 15.5 %copy-start = (bf16[16,288,128]{2,1,0:T(8,128)(2,1)}, bf16[16,288,128]{2,1,0:T(8,128)(2,1)S(1)}, u32[]{:S(2)}) copy-start(bf16[16,288,128]{2,1,0:T(8,128)(2,1)S(1)} %all-to-all-done.3.src) | copy-start | bytes 3538948
  174.0 10.8 %all-to-all-start.4 = ((bf16[8,6,1536]{2,1,0:T(8,128)(2,1)}), bf16[8,6,1536]{2,1,0:T(8,128)(2,1)S(1)}, u32[]{:S(2)}, u32[]{:S(2)}) async-start(bf16[8,6,1536]{2,1,0:T(8,128)(2,1)} %reshape.26), calls=%async_computation.6 | async-start | bytes 393216 | tf_op jit(solution)/shard_map/all_to_all | solution.py:280
Sparse Core Ops, SparseCore 0:
  62.9 32.7 all-gather.1
  109.9 23.2 reduce-scatter.4
  136.4 41.7 reduce-scatter.2
